TPU v7x, 512 devices: a whole 4x4x16 slice. The times are simulated.
512 devices in a mesh: rep: 8 (over y, x_hi), fsdp: 64 (over z, x_lo, core).
Axes of the slice: x: 4 (x_hi: 2, x_lo: 2; x = x_hi * 2 + x_lo), y: 4, z: 16, core: 2. Of those that a mesh axis runs over, the one named last changes fastest.
Arguments:
- activations: bfloat16 [8, 40960, 3072], P('rep', 'fsdp'), may hold values from -16 to 16
- cotangent: bfloat16 [8, 40960, 256], P('rep', 'fsdp'), may hold values from -0.03125 to 0.03125
- momentum: float32 [8, 3072, 256], P('rep', 'fsdp'), may hold values from -6 to 6
- components: int32 [8, 3072, 4, 8], P('rep', 'fsdp'), may hold values from 0 to 63, as said below
Outputs:
- update: float32 [3072, 256], P('fsdp')
- renewed: float32 [8, 3072, 256], P('rep', 'fsdp')
Inputs may be any that keep to these rules, and one draw needn't show every extreme that they name: The 8 components listed for one span are distinct.
All inputs are finite; a program needn't handle non-finite values.
Results may differ from a plain program's by a relative error of at most 0.0003.
Values sent between devices are 32-bit elements; how exact they have to be, the bound alone decides.
No kernel may reach another device: no remote copies, remote signals or barrier semaphores. Data moves between devices by JAX's collectives and lax.ppermute only.
A program may use at most 64 MiB of HBM per device.

v0:
```python
import math

import jax
import jax.numpy as jnp
from jax import lax
from jax.sharding import PartitionSpec as P

SPAN = 64


beta_decay = 0.999
highest = lax.Precision.HIGHEST


def dct_table(length_span):
    frequency = jnp.arange(length_span, dtype=jnp.float32)[:, None]
    position = jnp.arange(length_span, dtype=jnp.float32)[None, :]
    cosine_raw = jnp.cos(math.pi * (2.0 * position + 1.0) * frequency / (2.0 * length_span))
    normalizer = jnp.where(
        frequency == 0.0, math.sqrt(1.0 / length_span), math.sqrt(2.0 / length_span)
    )
    return cosine_raw * normalizer


def encode(gradient, moment, chosen, cosines):
    row_count, col_count = gradient.shape
    moment_new = beta_decay * moment + gradient
    spans = moment_new.reshape(row_count, col_count // SPAN, SPAN)
    spectrum = jnp.einsum("rcn,kn->rck", spans, cosines, precision=highest)
    onehot = (chosen[..., None] == jnp.arange(SPAN, dtype=jnp.int32)).astype(jnp.float32)
    amounts = jnp.einsum("rcjk,rck->rcj", onehot, spectrum, precision=highest)
    retained = jnp.einsum("rcjk,rcj->rck", onehot, amounts, precision=highest)
    restored = jnp.einsum("rck,kn->rcn", retained, cosines, precision=highest).reshape(
        row_count, col_count
    )
    return (moment_new - restored, amounts, retained)


def shards(activations, cotangent, momentum, components):
    cosines = dct_table(SPAN)
    inputs_local = activations[0]
    cot_local = cotangent[0]
    moment = momentum[0]
    chosen = components[0]
    row_count = moment.shape[0]
    gradient = lax.psum_scatter(
        lax.dot_general(
            inputs_local, cot_local, (((0,), (0,)), ((), ())), preferred_element_type=jnp.float32
        ),
        "fsdp",
        scatter_dimension=0,
        tiled=True,
    )
    renewed, amounts, retained = encode(gradient, moment, chosen, cosines)
    amount_piece = lax.all_gather(amounts[None], "rep", axis=0, tiled=True)
    index_piece = lax.all_gather(chosen[None], "rep", axis=0, tiled=True)
    onehot = (index_piece[..., None] == jnp.arange(SPAN, dtype=jnp.int32)).astype(jnp.float32)
    summed = jnp.einsum("qrcjk,qrcj->rck", onehot, amount_piece, precision=highest)
    group_count = lax.axis_size("rep")
    update = (
        jnp.einsum("rck,kn->rcn", summed, cosines, precision=highest).reshape(row_count, -1)
        / group_count
    )
    return (update, renewed[None])


def solution(mesh):
    return jax.shard_map(
        shards,
        mesh=mesh,
        in_specs=(
            P("rep", "fsdp", None),
            P("rep", "fsdp", None),
            P("rep", "fsdp", None),
            P("rep", "fsdp", None, None),
        ),
        out_specs=(P("fsdp", None), P("rep", "fsdp", None)),
        check_vma=False,
    )
```

profile of v0, /device:TPU:4, one launch (start us, length us, event | category | flops | bytes accessed | tf_op | source)
XLA Modules:
  0.0 304.0 jit_solution(8798530618286367822)
XLA Ops:
  7.2 0.0 copy-start
  7.2 0.0 copy-start.1
  7.2 0.0 reduce-scatter.2.cloned.1.call-start
  7.2 0.9 copy-done
  8.1 5.2 %fusion.1 = f32[3072,256]{1,0:T(8,128)} fusion(bf16[1,640,3072]{2,1,0:T(8,128)(2,1)} %param.4, bf16[1,640,256]{2,1,0:T(8,128)(2,1)S(1)} %copy-done), kind=kOutput, calls=%fused_computation.2 | convolution fusion | flops 1006632960 | bytes 7405568 | tf_op jit(solution)/shard_map/dot_general | solution.py:47
  13.3 0.0 copy-start.2
  13.3 0.0 reduce-scatter.2.cloned.1.call-update
  13.4 0.0 copy-done.1
  13.4 0.1 copy.14
  13.5 34.8 %all_gather.6 = s32[8,48,4,8]{1,3,2,0:T(8,128)S(1)} all-gather(s32[1,48,4,8]{1,3,2,0:T(8,128)S(1)} %copy-done.1), channel_id=1, replica_groups=mesh['rep'=8,'fsdp'=64] {'rep'}, dimensions={0}, use_global_device_ids=true | all-gather | bytes 55296 | tf_op jit(solution)/shard_map/all_gather | solution.py:56
  48.3 0.3 copy.13
  48.6 199.7 %reduce-scatter.2.cloned.1.call-done = f32[48,256]{1,0:T(8,128)} async-done(((f32[3072,256]{1,0:T(8,128)}), f32[48,256]{1,0:T(8,128)}) %reduce-scatter.2.cloned.1.call-update) | async-done | bytes 49168 | tf_op jit(solution)/shard_map/reduce_scatter | solution.py:46
  248.3 0.0 copy-done.2
  248.3 0.8 bitcast_add_fusion
  249.1 0.1 reshape.33
  249.2 0.4 convolution_bitcast_fusion
  249.6 0.9 fusion.5
  250.4 0.8 fusion.4
  251.3 0.4 fusion.9
  251.7 0.1 reshape.34
  251.8 0.6 subtract_bitcast_fusion
  252.4 36.2 %all-gather = f32[384,4,8]{2,1,0:T(4,128)S(1)} all-gather(f32[48,4,8]{2,1,0:T(4,128)S(1)} %bitcast.40), channel_id=2, replica_groups=mesh['rep'=8,'fsdp'=64] {'rep'}, dimensions={0}, use_global_device_ids=true | all-gather | bytes 55296 | tf_op jit(solution)/shard_map/all_gather | solution.py:55
  288.6 7.4 %fusion = f32[48,4,1,64,1]{3,2,1,0,4:T(1,128)S(1)} fusion(f32[8,48,4,8,1]{3,4,2,1,0:T(1,128)S(1)} %bitcast.39, s32[8,48,4,8]{3,2,1,0:T(4,128)S(1)} %copy.13), kind=kOutput, calls=%fused_computation.1 | convolution fusion | flops 10223616 | bytes 147456 | tf_op jit(solution)/shard_map/qrcjk,qrcj->rck/dot_general | solution.py:58
  296.0 0.4 convolution_multiply_fusion
  296.4 0.7 div.22
  (3 shorter events, 0.1 us)
Async XLA Ops:
  7.2 1.0 copy-start
  7.2 6.2 %copy-start.1 = (s32[1,48,4,8]{1,3,2,0:T(8,128)S(1)}, s32[1,48,4,8]{1,3,2,0:T(8,128)}, u32[]{:S(2)}) copy-start(s32[1,48,4,8]{1,3,2,0:T(8,128)} %param.7) | copy-start | bytes 18436
  7.2 241.1 %reduce-scatter.2.cloned.1.call-start = ((), (), s32[]{:S(2)}) async-start(), calls=%async_computation.1 | async-start | bytes 3194880 | tf_op jit(solution)/shard_map/reduce_scatter | solution.py:46
  13.3 234.9 %copy-start.2 = (f32[1,48,256]{2,1,0:T(8,128)S(1)}, f32[1,48,256]{2,1,0:T(8,128)}, u32[]{:S(2)}) copy-start(f32[1,48,256]{2,1,0:T(8,128)} %param.6) | copy-start | bytes 147460
Sparse Core Ops, SparseCore 0:
  13.5 234.7 reduce-scatter.1
where the time goes:
time: 304 us
  waiting for transfers between devices  200 us (66%)
  blocking collectives  71 us (23%)
  matrix products  15.3 us (5%)
  between operations  14.1 us (5%)
    reduce_scatter x1, waiting for transfers between devices, shards(): lax.psum_scatter(lax.dot_general(inputs_local, cot_local, (((0,), (0,)),...  200 us
    all_gather x1, blocking collectives, shards(): amount_piece = lax.all_gather(amounts[None], 'rep', axis=0, tiled=True)  36.2 us
    all_gather x1, blocking collectives, shards(): index_piece = lax.all_gather(chosen[None], 'rep', axis=0, tiled=True)  34.8 us
    dot_general x1, matrix products, shards(): jnp.einsum('qrcjk,qrcj->rck', onehot, amount_piece, precision=highest)  7.36 us
  transfers between devices with their start and end apart: 1, of which 1 were waited for; matrix products, arithmetic and copies ran while one was open for 0% of the time, Pallas kernels for 0%

commit v1 on v0

v1 whole, which is shorter than its diff:
```python
import math

import jax
import jax.numpy as jnp
import numpy as np
from jax import lax
from jax.experimental import pallas as pl
from jax.experimental.pallas import tpu as pltpu
from jax.sharding import PartitionSpec as P

SPAN = 64
PAIRS = 8
beta_decay = 0.999
highest = lax.Precision.HIGHEST


def span_tables(cols):
    frequency = np.arange(SPAN, dtype=np.float64)[:, None]
    position = np.arange(SPAN, dtype=np.float64)[None, :]
    cosines = np.cos(math.pi * (2.0 * position + 1.0) * frequency / (2.0 * SPAN))
    cosines *= np.where(frequency == 0.0, math.sqrt(1.0 / SPAN), math.sqrt(2.0 / SPAN))
    return np.kron(np.eye(cols // SPAN), cosines.T).astype(np.float32)


def place(index):
    z = index // 4
    pair, bit = z // 2, z % 2
    return pair, bit ^ (pair // 4), (index // 2) % 2, index % 2


def index_of(pair, group, x, core):
    return (2 * pair + (group ^ (pair // 4))) * 4 + x * 2 + core


def swapped(dgroup, dx, dcore):
    pairs = []
    for f in range(64):
        pair, group, x, core = place(f)
        pairs.append((f, index_of(pair, group ^ dgroup, x ^ dx, core ^ dcore)))
    return pairs


def partial_kernel(acts_ref, cot_ref, out_ref):
    step = pl.program_id(0)
    _, group, x, core = place(lax.axis_index("fsdp"))
    product = lax.dot_general(
        acts_ref[...], cot_ref[...], (((0,), (0,)), ((), ())), preferred_element_type=jnp.float32
    )
    rows = product.shape[0] // 8
    for bit in range(2):
        for to_x in range(2):
            for to_core in range(2):
                at = (bit * 4 + to_x * 2 + to_core) * rows
                out_ref[to_core ^ core, bit ^ (step // 4) ^ group, to_x ^ x, 0] = product[at : at + rows]


def partials(acts, cot):
    tokens, dim = acts.shape
    cols = cot.shape[1]
    width = dim // PAIRS
    return pl.pallas_call(
        partial_kernel,
        grid=(PAIRS,),
        in_specs=[
            pl.BlockSpec((tokens, width), lambda p: (0, p)),
            pl.BlockSpec((tokens, cols), lambda p: (0, 0)),
        ],
        out_specs=pl.BlockSpec((2, 2, 2, 1, width // 8, cols), lambda p: (0, 0, 0, p, 0, 0)),
        out_shape=jax.ShapeDtypeStruct((2, 2, 2, PAIRS, width // 8, cols), jnp.float32),
        compiler_params=pltpu.CompilerParams(vmem_limit_bytes=48 << 20),
    )(acts, cot)


def encode_kernel(pieces_ref, moment_ref, chosen_ref, table_ref, renewed_ref, copies_ref):
    moment_new = beta_decay * moment_ref[...] + jnp.sum(pieces_ref[...], axis=0)
    rows, cols = moment_new.shape
    spans, kept, _ = chosen_ref.shape
    spectrum = jnp.dot(moment_new, table_ref[...], precision=highest, preferred_element_type=jnp.float32)
    component = lax.broadcasted_iota(jnp.int32, (SPAN, rows), 0)
    masks = []
    for c in range(spans):
        hit = component == chosen_ref[c, 0:1, :]
        for j in range(1, kept):
            hit = hit | (component == chosen_ref[c, j : j + 1, :])
        masks.append(jnp.where(hit, 1.0, 0.0))
    mask = jnp.concatenate(masks, axis=0).T
    retained = jnp.where(mask > 0.5, spectrum, 0.0)
    restored = lax.dot_general(
        retained, table_ref[...], (((1,), (1,)), ((), ())), precision=highest, preferred_element_type=jnp.float32
    )
    renewed_ref[...] = moment_new - restored
    copies_ref[...] = jnp.broadcast_to(restored, copies_ref.shape)


def encode(pieces, moment, chosen, copies):
    rows, cols = moment.shape
    return pl.pallas_call(
        encode_kernel,
        out_shape=(
            jax.ShapeDtypeStruct((rows, cols), jnp.float32),
            jax.ShapeDtypeStruct((copies, rows, cols), jnp.float32),
        ),
    )(pieces, moment, chosen, jnp.asarray(span_tables(cols)))


def shards(activations, cotangent, momentum, components):
    groups = lax.axis_size("rep")
    part = partials(activations[0], cotangent[0])
    mine = part[0] + lax.ppermute(part[1], "fsdp", swapped(0, 0, 1))
    both = lax.ppermute(mine[1, 1], "fsdp", swapped(1, 1, 0))
    along_x = lax.ppermute(mine[0, 1], "fsdp", swapped(0, 1, 0))
    along_z = lax.ppermute(mine[1, 0], "fsdp", swapped(1, 0, 0))
    mine = mine[0, 0] + both + along_x + along_z
    members = [
        [index_of(pair, group, x, core) for pair in range(PAIRS)]
        for group in range(2)
        for x in range(2)
        for core in range(2)
    ]
    pieces = lax.all_to_all(mine, "fsdp", 0, 0, axis_index_groups=members)
    chosen = components[0].transpose(1, 2, 0)
    renewed, copies = encode(pieces, momentum[0], chosen, groups)
    restored = lax.all_to_all(copies, "rep", 0, 0)
    update = jnp.sum(restored, axis=0) / groups
    return (update, renewed[None])


def solution(mesh):
    return jax.shard_map(
        shards,
        mesh=mesh,
        in_specs=(
            P("rep", "fsdp", None),
            P("rep", "fsdp", None),
            P("rep", "fsdp", None),
            P("rep", "fsdp", None, None),
        ),
        out_specs=(P("fsdp", None), P("rep", "fsdp", None)),
        check_vma=False,
    )
```

time: 304 us -> 96.1 us (0.32)
  the two profiles are of different devices: /device:TPU:4 before, /device:TPU:32 now
where the time goes in v1:
time: 96.1 us; the launch traced here: 95.6 us
  blocking collectives  53.3 us (55%)
  waiting for transfers between devices  15.9 us (17%)
  starting transfers between devices  14.6 us (15%)
  Pallas kernels  8.89 us (9%)
  local copies, waits for them, and re-layouts  1.16 us (1%)
  other arithmetic  0.98 us (1%)
    all_to_all x1, blocking collectives, shards(): pieces = lax.all_to_all(mine, 'fsdp', 0, 0, axis_index_groups=members)  36.7 us
    all_to_all x1, blocking collectives, shards(): restored = lax.all_to_all(copies, 'rep', 0, 0)  16.6 us
    ppermute x1, waiting for transfers between devices, shards(): along_z = lax.ppermute(mine[1, 0], 'fsdp', swapped(1, 0, 0))  10.5 us
    ppermute x1, starting transfers between devices, shards(): along_z = lax.ppermute(mine[1, 0], 'fsdp', swapped(1, 0, 0))  6.37 us
    pallas_call x1, Pallas kernels, partials(): pl.pallas_call(partial_kernel, grid=(PAIRS,), in_specs=[pl.BlockSpec((tok...  6.23 us
    ppermute x1, waiting for transfers between devices, shards(): mine = part[0] + lax.ppermute(part[1], 'fsdp', swapped(0, 0, 1))  3.38 us
    ppermute x1, starting transfers between devices, shards(): along_x = lax.ppermute(mine[0, 1], 'fsdp', swapped(0, 1, 0))  3.37 us
    ppermute x1, starting transfers between devices, shards(): both = lax.ppermute(mine[1, 1], 'fsdp', swapped(1, 1, 0))  2.95 us
  transfers between devices with their start and end apart: 4, of which 3 were waited for; matrix products, arithmetic and copies ran while one was open for 0% of the time, Pallas kernels for 0%

profile of v1, /device:TPU:32, one launch (start us, length us, event | category | flops | bytes accessed | tf_op | source)
XLA Modules:
  0.0 95.6 jit_solution(6152810354944027684)
XLA Ops:
  0.6 0.0 copy-start
  0.6 1.0 %copy-done = bf16[1,640,256]{2,1,0:T(8,128)(2,1)S(1)} copy-done((bf16[1,640,256]{2,1,0:T(8,128)(2,1)S(1)}, bf16[1,640,256]{2,1,0:T(8,128)(2,1)}, u32[]{:S(2)}) %copy-start) | copy-done | bytes 327704
  1.6 6.2 %shard_map.68 = f32[2,2,2,8,48,256]{5,4,3,2,1,0:T(8,128)S(1)} custom-call(bf16[640,3072]{1,0:T(8,128)(2,1)} %bitcast.28, bf16[640,256]{1,0:T(8,128)(2,1)S(1)} %bitcast.27), custom_call_target="tpu_custom_call" | custom-call | tf_op jit(solution)/shard_map/pallas_call | solution.py:61
  7.8 0.1 slice_bitcast_fusion
  8.0 1.9 %collective-permute-start = (f32[2,2,8,48,256]{4,3,2,1,0:T(8,128)S(1)}, f32[2,2,8,48,256]{4,3,2,1,0:T(8,128)S(1)}, u32[]{:S(2)}, u32[]{:S(2)}) collective-permute-start(f32[2,2,8,48,256]{4,3,2,1,0:T(8,128)S(1)} %slice_bitcast_fusion), channel_id=1, source_target_pairs={{0,1},{1,0},{2,3},{3,2},{4,5},{5,4},{6,7},{7,6},{8,9},{9,8},{10,11... | collective-permute-start | bytes 4718600 | tf_op jit(solution)/shard_map/ppermute | solution.py:109
  9.9 3.4 %collective-permute-done = f32[2,2,8,48,256]{4,3,2,1,0:T(8,128)S(1)} collective-permute-done((f32[2,2,8,48,256]{4,3,2,1,0:T(8,128)S(1)}, f32[2,2,8,48,256]{4,3,2,1,0:T(8,128)S(1)}, u32[]{:S(2)}, u32[]{:S(2)}) %collective-permute-start) | collective-permute-done | bytes 1572896 | tf_op jit(solution)/shard_map/ppermute | solution.py:109
  13.3 0.2 fusion
  13.5 0.1 slice_bitcast_fusion.4
  13.6 2.9 %collective-permute-start.1 = (f32[8,48,256]{2,1,0:T(8,128)S(1)}, f32[8,48,256]{2,1,0:T(8,128)S(1)}, u32[]{:S(2)}, u32[]{:S(2)}) collective-permute-start(f32[8,48,256]{2,1,0:T(8,128)S(1)} %get-tuple-element.6), channel_id=1, source_target_pairs={{0,6},{1,7},{2,4},{3,5},{4,2},{5,3},{6,0},{7,1},{8,14},{9,15},{10,... | collective-permute-start | bytes 1179656 | tf_op jit(solution)/shard_map/ppermute | solution.py:110
  16.5 6.4 %collective-permute-start.3 = (f32[8,48,256]{2,1,0:T(8,128)S(1)}, f32[8,48,256]{2,1,0:T(8,128)S(1)}, u32[]{:S(2)}, u32[]{:S(2)}) collective-permute-start(f32[8,48,256]{2,1,0:T(8,128)S(1)} %get-tuple-element.7), channel_id=1, source_target_pairs={{0,4},{1,5},{2,6},{3,7},{4,0},{5,1},{6,2},{7,3},{8,12},{9,13},{10,... | collective-permute-start | bytes 1179656 | tf_op jit(solution)/shard_map/ppermute | solution.py:112
  22.9 3.4 %collective-permute-start.2 = (f32[8,48,256]{2,1,0:T(8,128)S(1)}, f32[8,48,256]{2,1,0:T(8,128)S(1)}, u32[]{:S(2)}, u32[]{:S(2)}) collective-permute-start(f32[8,48,256]{2,1,0:T(8,128)S(1)} %get-tuple-element.8), channel_id=1, source_target_pairs={{0,2},{1,3},{2,0},{3,1},{4,6},{5,7},{6,4},{7,5},{8,10},{9,11},{10,... | collective-permute-start | bytes 1179656 | tf_op jit(solution)/shard_map/ppermute | solution.py:111
  26.3 2.0 %collective-permute-done.1 = f32[8,48,256]{2,1,0:T(8,128)S(1)} collective-permute-done((f32[8,48,256]{2,1,0:T(8,128)S(1)}, f32[8,48,256]{2,1,0:T(8,128)S(1)}, u32[]{:S(2)}, u32[]{:S(2)}) %collective-permute-start.1) | collective-permute-done | bytes 393248 | tf_op jit(solution)/shard_map/ppermute | solution.py:110
  28.3 10.5 %collective-permute-done.3 = f32[8,48,256]{2,1,0:T(8,128)S(1)} collective-permute-done((f32[8,48,256]{2,1,0:T(8,128)S(1)}, f32[8,48,256]{2,1,0:T(8,128)S(1)}, u32[]{:S(2)}, u32[]{:S(2)}) %collective-permute-start.3) | collective-permute-done | bytes 393248 | tf_op jit(solution)/shard_map/ppermute | solution.py:112
  38.9 0.0 collective-permute-done.2
  38.9 0.1 fusion.3
  39.0 36.7 %all_to_all.10.pieces_ref = f32[8,48,256]{2,1,0:T(8,128)} all-to-all(f32[8,48,256]{2,1,0:T(8,128)S(1)} %fusion.3), channel_id=1, replica_groups={{0,8,16,24,36,44,52,60},{1,9,17,25,37,45,53,61},{2,10,18,26,38,46,54,62..., dimensions={0} | all-to-all | bytes 786432 | tf_op jit(solution)/shard_map/all_to_all | solution.py:120
  75.7 2.7 %shard_map.69 = (f32[48,256]{1,0:T(8,128)}, f32[8,48,256]{2,1,0:T(8,128)}) custom-call(f32[8,48,256]{2,1,0:T(8,128)} %all_to_all.10.pieces_ref, f32[48,256]{1,0:T(8,128)} %bitcast.29, s32[4,8,48]{2,1,0:T(8,128)} %bitcast.30, f32[256,256]{1,0:T(8,128)} %constant.7.clone.table_ref), custom_call_target="tpu_custom_call" | custom-call | tf_op jit(solution)/shard_map/pallas_call | solution.py:97
  78.3 16.6 %all_to_all.11 = f32[8,48,256]{2,1,0:T(8,128)S(1)} all-to-all(f32[8,48,256]{2,1,0:T(8,128)} %get-tuple-element.4), channel_id=1, replica_groups=mesh['rep'=8,'fsdp'=64] {'rep'}, dimensions={0} | all-to-all | bytes 786432 | tf_op jit(solution)/shard_map/all_to_all | solution.py:123
  94.9 0.6 broadcast_multiply_fusion
  (1 shorter events, 0.0 us)
Async XLA Ops:
  0.6 1.0 %copy-start = (bf16[1,640,256]{2,1,0:T(8,128)(2,1)S(1)}, bf16[1,640,256]{2,1,0:T(8,128)(2,1)}, u32[]{:S(2)}) copy-start(bf16[1,640,256]{2,1,0:T(8,128)(2,1)} %param.6) | copy-start | bytes 983044
  8.0 5.3 %collective-permute-start = (f32[2,2,8,48,256]{4,3,2,1,0:T(8,128)S(1)}, f32[2,2,8,48,256]{4,3,2,1,0:T(8,128)S(1)}, u32[]{:S(2)}, u32[]{:S(2)}) collective-permute-start(f32[2,2,8,48,256]{4,3,2,1,0:T(8,128)S(1)} %slice_bitcast_fusion), channel_id=1, source_target_pairs={{0,1},{1,0},{2,3},{3,2},{4,5},{5,4},{6,7},{7,6},{8,9},{9,8},{10,11... | collective-permute-start | bytes 4718600 | tf_op jit(solution)/shard_map/ppermute | solution.py:109
  13.6 14.8 %collective-permute-start.1 = (f32[8,48,256]{2,1,0:T(8,128)S(1)}, f32[8,48,256]{2,1,0:T(8,128)S(1)}, u32[]{:S(2)}, u32[]{:S(2)}) collective-permute-start(f32[8,48,256]{2,1,0:T(8,128)S(1)} %get-tuple-element.6), channel_id=1, source_target_pairs={{0,6},{1,7},{2,4},{3,5},{4,2},{5,3},{6,0},{7,1},{8,14},{9,15},{10,... | collective-permute-start | bytes 1179656 | tf_op jit(solution)/shard_map/ppermute | solution.py:110
  16.5 22.3 %collective-permute-start.3 = (f32[8,48,256]{2,1,0:T(8,128)S(1)}, f32[8,48,256]{2,1,0:T(8,128)S(1)}, u32[]{:S(2)}, u32[]{:S(2)}) collective-permute-start(f32[8,48,256]{2,1,0:T(8,128)S(1)} %get-tuple-element.7), channel_id=1, source_target_pairs={{0,4},{1,5},{2,6},{3,7},{4,0},{5,1},{6,2},{7,3},{8,12},{9,13},{10,... | collective-permute-start | bytes 1179656 | tf_op jit(solution)/shard_map/ppermute | solution.py:112
  22.9 15.9 %collective-permute-start.2 = (f32[8,48,256]{2,1,0:T(8,128)S(1)}, f32[8,48,256]{2,1,0:T(8,128)S(1)}, u32[]{:S(2)}, u32[]{:S(2)}) collective-permute-start(f32[8,48,256]{2,1,0:T(8,128)S(1)} %get-tuple-element.8), channel_id=1, source_target_pairs={{0,2},{1,3},{2,0},{3,1},{4,6},{5,7},{6,4},{7,5},{8,10},{9,11},{10,... | collective-permute-start | bytes 1179656 | tf_op jit(solution)/shard_map/ppermute | solution.py:111

commit v2 on v1

v2 whole, which is shorter than its diff:
```python
import math

import jax
import jax.numpy as jnp
import numpy as np
from jax import lax
from jax.experimental import pallas as pl
from jax.experimental.pallas import tpu as pltpu
from jax.sharding import PartitionSpec as P

SPAN = 64
PAIRS = 8
beta_decay = 0.999
highest = lax.Precision.HIGHEST


def span_tables(cols):
    frequency = np.arange(SPAN, dtype=np.float64)[:, None]
    position = np.arange(SPAN, dtype=np.float64)[None, :]
    cosines = np.cos(math.pi * (2.0 * position + 1.0) * frequency / (2.0 * SPAN))
    cosines *= np.where(frequency == 0.0, math.sqrt(1.0 / SPAN), math.sqrt(2.0 / SPAN))
    return np.kron(np.eye(cols // SPAN), cosines.T).astype(np.float32)


def place(index):
    z = index // 4
    pair, bit = z // 2, z % 2
    return pair, bit ^ (pair // 4), (index // 2) % 2, index % 2


def index_of(pair, group, x, core):
    return (2 * pair + (group ^ (pair // 4))) * 4 + x * 2 + core


def swapped(dgroup, dx, dcore):
    pairs = []
    for f in range(64):
        pair, group, x, core = place(f)
        pairs.append((f, index_of(pair, group ^ dgroup, x ^ dx, core ^ dcore)))
    return pairs


def in_hbm(array):
    return pltpu.with_memory_space_constraint(array, pltpu.HBM)


def partial_kernel(
    acts_hbm, cot_hbm, chosen_hbm, out_ref, mask_ref, acts, cot, chosen_ref, acts_sem, cot_sem, chosen_sem
):
    copy_chosen = pltpu.make_async_copy(chosen_hbm, chosen_ref, chosen_sem)
    copy_chosen.start()
    copy_cot = pltpu.make_async_copy(cot_hbm, cot, cot_sem)
    copy_cot.start()
    copy_acts = pltpu.make_async_copy(acts_hbm, acts, acts_sem)
    copy_acts.start()
    spans, kept, rows = chosen_ref.shape
    copy_chosen.wait()
    component = lax.broadcasted_iota(jnp.int32, (SPAN, rows), 0)
    masks = []
    for c in range(spans):
        hit = component == chosen_ref[c, 0:1, :]
        for j in range(1, kept):
            hit = hit | (component == chosen_ref[c, j : j + 1, :])
        masks.append(jnp.where(hit, 1.0, 0.0))
    mask_ref[...] = jnp.concatenate(masks, axis=0).T
    _, group, x, core = place(lax.axis_index("fsdp"))
    copy_cot.wait()
    turned = cot[...].T
    copy_acts.wait()
    width = acts.shape[1] // 4
    for step in range(4):
        product = jnp.dot(
            turned, acts[:, step * width : (step + 1) * width], preferred_element_type=jnp.float32
        ).T
        for at in range(0, width, rows):
            pair, bit, to_x, to_core = place((step * width + at) // rows)
            out_ref[to_core ^ core, pair // 4, to_x ^ x, bit ^ group, pair % 4] = product[at : at + rows]


def partials(acts, cot, chosen):
    dim, cols = acts.shape[1], cot.shape[1]
    rows = chosen.shape[2]
    return pl.pallas_call(
        partial_kernel,
        in_specs=[
            pl.BlockSpec(memory_space=pl.ANY),
            pl.BlockSpec(memory_space=pl.ANY),
            pl.BlockSpec(memory_space=pl.ANY),
        ],
        out_shape=(
            jax.ShapeDtypeStruct((2, 2, 2, 2, PAIRS // 2, dim // (8 * PAIRS), cols), jnp.float32),
            jax.ShapeDtypeStruct((rows, cols), jnp.float32),
        ),
        scratch_shapes=[
            pltpu.VMEM(acts.shape, acts.dtype),
            pltpu.VMEM(cot.shape, cot.dtype),
            pltpu.VMEM(chosen.shape, chosen.dtype),
            pltpu.SemaphoreType.DMA,
            pltpu.SemaphoreType.DMA,
            pltpu.SemaphoreType.DMA,
        ],
        compiler_params=pltpu.CompilerParams(vmem_limit_bytes=40 << 20),
    )(in_hbm(acts), in_hbm(cot), in_hbm(chosen))


def encode_kernel(pieces_ref, moment_ref, mask_ref, table_ref, renewed_ref, copies_ref):
    moment_new = beta_decay * moment_ref[...] + jnp.sum(pieces_ref[...], axis=0)
    spectrum = jnp.dot(moment_new, table_ref[...], precision=highest, preferred_element_type=jnp.float32)
    retained = jnp.where(mask_ref[...] > 0.5, spectrum, 0.0)
    restored = lax.dot_general(
        retained, table_ref[...], (((1,), (1,)), ((), ())), precision=highest, preferred_element_type=jnp.float32
    )
    renewed_ref[...] = moment_new - restored
    copies_ref[...] = jnp.broadcast_to(restored, copies_ref.shape)


def encode(pieces, moment, mask, copies):
    rows, cols = moment.shape
    return pl.pallas_call(
        encode_kernel,
        out_shape=(
            jax.ShapeDtypeStruct((rows, cols), jnp.float32),
            jax.ShapeDtypeStruct((copies, rows, cols), jnp.float32),
        ),
    )(pieces, moment, mask, jnp.asarray(span_tables(cols)))


def shards(activations, cotangent, momentum, components):
    groups = lax.axis_size("rep")
    part, mask = partials(activations[0], cotangent[0], components[0].transpose(1, 2, 0))
    first = part[0, 0] + lax.ppermute(part[1, 0], "fsdp", swapped(0, 0, 1))
    second = part[0, 1] + lax.ppermute(part[1, 1], "fsdp", swapped(0, 0, 1))
    first = first[0] + lax.ppermute(first[1], "fsdp", swapped(0, 1, 0))
    second = second[:, 0] + lax.ppermute(second[:, 1], "fsdp", swapped(1, 0, 0))
    first = first[0] + lax.ppermute(first[1], "fsdp", swapped(1, 0, 0))
    second = second[0] + lax.ppermute(second[1], "fsdp", swapped(0, 1, 0))
    mine = jnp.concatenate([first, second])
    members = [
        [index_of(pair, group, x, core) for pair in range(PAIRS)]
        for group in range(2)
        for x in range(2)
        for core in range(2)
    ]
    pieces = lax.all_to_all(mine, "fsdp", 0, 0, axis_index_groups=members)
    renewed, copies = encode(pieces, momentum[0], mask, groups)
    restored = lax.all_to_all(copies, "rep", 0, 0)
    update = jnp.sum(restored, axis=0) / groups
    return (update, renewed[None])


def solution(mesh):
    return jax.shard_map(
        shards,
        mesh=mesh,
        in_specs=(
            P("rep", "fsdp", None),
            P("rep", "fsdp", None),
            P("rep", "fsdp", None),
            P("rep", "fsdp", None, None),
        ),
        out_specs=(P("fsdp", None), P("rep", "fsdp", None)),
        check_vma=False,
    )
```

time: 96.1 us -> 90.5 us (0.942)
  the two profiles are of different devices: /device:TPU:32 before, /device:TPU:2 now
where the time goes in v2:
time: 90.5 us; the launch traced here: 90.1 us
  blocking collectives  49.3 us (54%)
  starting transfers between devices  18.3 us (20%)
  waiting for transfers between devices  13.9 us (15%)
  Pallas kernels  6.45 us (7%)
  other arithmetic  1.05 us (1%)
    all_to_all x1, blocking collectives, shards(): pieces = lax.all_to_all(mine, 'fsdp', 0, 0, axis_index_groups=members)  33.7 us
    all_to_all x1, blocking collectives, shards(): restored = lax.all_to_all(copies, 'rep', 0, 0)  15.6 us
    ppermute x1, starting transfers between devices, shards(): first = first[0] + lax.ppermute(first[1], 'fsdp', swapped(0, 1, 0))  7.82 us
    ppermute x1, waiting for transfers between devices, shards(): first = first[0] + lax.ppermute(first[1], 'fsdp', swapped(0, 1, 0))  7.19 us
    pallas_call x1, Pallas kernels, partials(): pl.pallas_call(partial_kernel, in_specs=[pl.BlockSpec(memory_space=pl.ANY...  3.81 us
    ppermute x1, waiting for transfers between devices, shards(): second = second[0] + lax.ppermute(second[1], 'fsdp', swapped(0, 1, 0))  2.88 us
    pallas_call x1, Pallas kernels, encode(): pl.pallas_call(encode_kernel, out_shape=(jax.ShapeDtypeStruct((rows, cols...  2.64 us
    ppermute x1, starting transfers between devices, shards(): second = part[0, 1] + lax.ppermute(part[1, 1], 'fsdp', swapped(0, 0, 1))  2.41 us
  transfers between devices with their start and end apart: 6, of which 4 were waited for; matrix products, arithmetic and copies ran while one was open for 1% of the time, Pallas kernels for 0%

profile of v2, /device:TPU:2, one launch (start us, length us, event | category | flops | bytes accessed | tf_op | source)
XLA Modules:
  0.0 90.1 jit_solution(3522396752210284109)
XLA Ops:
  0.6 3.8 %shard_map.68 = (f32[2,2,2,2,4,48,256]{6,5,4,3,2,1,0:T(8,128)S(1)}, f32[48,256]{1,0:T(8,128)S(1)}) custom-call(bf16[640,3072]{1,0:T(8,128)(2,1)} %bitcast.41, bf16[640,256]{1,0:T(8,128)(2,1)} %bitcast.42, s32[4,8,48]{2,1,0:T(8,128)} %bitcast.44), custom_call_target="tpu_custom_call" | custom-call | tf_op jit(solution)/shard_map/pallas_call | solution.py:83
  4.5 0.0 copy-start
  4.5 0.1 slice_bitcast_fusion.2
  4.5 1.9 %collective-permute-start = (f32[2,2,4,48,256]{4,3,2,1,0:T(8,128)S(1)}, f32[2,2,4,48,256]{4,3,2,1,0:T(8,128)S(1)}, u32[]{:S(2)}, u32[]{:S(2)}) collective-permute-start(f32[2,2,4,48,256]{4,3,2,1,0:T(8,128)S(1)} %slice_bitcast_fusion.2), channel_id=1, source_target_pairs={{0,1},{1,0},{2,3},{3,2},{4,5},{5,4},{6,7},{7,6},{8,9},{9,8},{10,11... | collective-permute-start | bytes 2359304 | tf_op jit(solution)/shard_map/ppermute | solution.py:131
  6.5 0.1 slice_bitcast_fusion
  6.5 2.4 %collective-permute-start.3 = (f32[2,2,4,48,256]{4,3,2,0,1:T(8,128)S(1)}, f32[2,2,4,48,256]{4,3,2,0,1:T(8,128)S(1)}, u32[]{:S(2)}, u32[]{:S(2)}) collective-permute-start(f32[2,2,4,48,256]{4,3,2,0,1:T(8,128)S(1)} %slice_bitcast_fusion), channel_id=1, source_target_pairs={{0,1},{1,0},{2,3},{3,2},{4,5},{5,4},{6,7},{7,6},{8,9},{9,8},{10,11... | collective-permute-start | bytes 2359304 | tf_op jit(solution)/shard_map/ppermute | solution.py:132
  8.9 0.0 collective-permute-done
  8.9 0.1 bitcast_add_fusion
  9.1 0.0 copy-done
  9.1 7.8 %collective-permute-start.1 = (f32[2,4,48,256]{3,2,1,0:T(8,128)S(1)}, f32[2,4,48,256]{3,2,1,0:T(8,128)S(1)}, u32[]{:S(2)}, u32[]{:S(2)}) collective-permute-start(f32[2,4,48,256]{3,2,1,0:T(8,128)S(1)} %slice_bitcast_fusion.5), channel_id=1, source_target_pairs={{0,2},{1,3},{2,0},{3,1},{4,6},{5,7},{6,4},{7,5},{8,10},{9,11},{10,... | collective-permute-start | bytes 1179656 | tf_op jit(solution)/shard_map/ppermute | solution.py:133
  16.9 0.0 collective-permute-done.3
  16.9 0.1 fusion
  17.1 1.9 %collective-permute-start.4 = (f32[2,4,48,256]{3,2,1,0:T(8,128)S(1)}, f32[2,4,48,256]{3,2,1,0:T(8,128)S(1)}, u32[]{:S(2)}, u32[]{:S(2)}) collective-permute-start(f32[2,4,48,256]{3,2,1,0:T(8,128)S(1)} %slice_bitcast_fusion.3), channel_id=1, source_target_pairs={{0,4},{1,5},{2,6},{3,7},{4,0},{5,1},{6,2},{7,3},{8,12},{9,13},{10,... | collective-permute-start | bytes 1179656 | tf_op jit(solution)/shard_map/ppermute | solution.py:134
  19.0 7.2 %collective-permute-done.1 = f32[2,4,48,256]{3,2,1,0:T(8,128)S(1)} collective-permute-done((f32[2,4,48,256]{3,2,1,0:T(8,128)S(1)}, f32[2,4,48,256]{3,2,1,0:T(8,128)S(1)}, u32[]{:S(2)}, u32[]{:S(2)}) %collective-permute-start.1) | collective-permute-done | bytes 393248 | tf_op jit(solution)/shard_map/ppermute | solution.py:133
  26.2 0.1 fusion.2
  26.3 1.9 %collective-permute-start.2 = (f32[4,48,256]{2,1,0:T(8,128)S(1)}, f32[4,48,256]{2,1,0:T(8,128)S(1)}, u32[]{:S(2)}, u32[]{:S(2)}) collective-permute-start(f32[4,48,256]{2,1,0:T(8,128)S(1)} %slice_bitcast_fusion.9), channel_id=1, source_target_pairs={{0,4},{1,5},{2,6},{3,7},{4,0},{5,1},{6,2},{7,3},{8,12},{9,13},{10,... | collective-permute-start | bytes 589832 | tf_op jit(solution)/shard_map/ppermute | solution.py:135
  28.2 1.5 %collective-permute-done.4 = f32[2,4,48,256]{3,2,1,0:T(8,128)S(1)} collective-permute-done((f32[2,4,48,256]{3,2,1,0:T(8,128)S(1)}, f32[2,4,48,256]{3,2,1,0:T(8,128)S(1)}, u32[]{:S(2)}, u32[]{:S(2)}) %collective-permute-start.4) | collective-permute-done | bytes 393248 | tf_op jit(solution)/shard_map/ppermute | solution.py:134
  29.7 0.1 fusion.1
  29.8 2.3 %collective-permute-start.5 = (f32[4,48,256]{2,1,0:T(8,128)S(1)}, f32[4,48,256]{2,1,0:T(8,128)S(1)}, u32[]{:S(2)}, u32[]{:S(2)}) collective-permute-start(f32[4,48,256]{2,1,0:T(8,128)S(1)} %slice_bitcast_fusion.7), channel_id=1, source_target_pairs={{0,2},{1,3},{2,0},{3,1},{4,6},{5,7},{6,4},{7,5},{8,10},{9,11},{10,... | collective-permute-start | bytes 589832 | tf_op jit(solution)/shard_map/ppermute | solution.py:136
  32.2 2.3 %collective-permute-done.2 = f32[4,48,256]{2,1,0:T(8,128)S(1)} collective-permute-done((f32[4,48,256]{2,1,0:T(8,128)S(1)}, f32[4,48,256]{2,1,0:T(8,128)S(1)}, u32[]{:S(2)}, u32[]{:S(2)}) %collective-permute-start.2) | collective-permute-done | bytes 196640 | tf_op jit(solution)/shard_map/ppermute | solution.py:135
  34.5 2.9 %collective-permute-done.5 = f32[4,48,256]{2,1,0:T(8,128)S(1)} collective-permute-done((f32[4,48,256]{2,1,0:T(8,128)S(1)}, f32[4,48,256]{2,1,0:T(8,128)S(1)}, u32[]{:S(2)}, u32[]{:S(2)}) %collective-permute-start.5) | collective-permute-done | bytes 196640 | tf_op jit(solution)/shard_map/ppermute | solution.py:136
  37.5 33.7 %all_to_all.10.pieces_ref = f32[8,48,256]{2,1,0:T(8,128)} all-to-all(f32[8,48,256]{2,1,0:T(8,128)S(1)} %pad_maximum_fusion), channel_id=1, replica_groups={{0,8,16,24,36,44,52,60},{1,9,17,25,37,45,53,61},{2,10,18,26,38,46,54,62..., dimensions={0} | all-to-all | bytes 786432 | tf_op jit(solution)/shard_map/all_to_all | solution.py:144
  71.1 2.6 %shard_map.69 = (f32[48,256]{1,0:T(8,128)}, f32[8,48,256]{2,1,0:T(8,128)}) custom-call(f32[8,48,256]{2,1,0:T(8,128)} %all_to_all.10.pieces_ref, f32[48,256]{1,0:T(8,128)} %bitcast.43, f32[48,256]{1,0:T(8,128)} %copy-done, f32[256,256]{1,0:T(8,128)} %constant.7.clone.table_ref), custom_call_target="tpu_custom_call" | custom-call | tf_op jit(solution)/shard_map/pallas_call | solution.py:119
  73.8 15.6 %all_to_all.11 = f32[8,48,256]{2,1,0:T(8,128)S(1)} all-to-all(f32[8,48,256]{2,1,0:T(8,128)} %get-tuple-element.8), channel_id=1, replica_groups=mesh['rep'=8,'fsdp'=64] {'rep'}, dimensions={0} | all-to-all | bytes 786432 | tf_op jit(solution)/shard_map/all_to_all | solution.py:146
  89.5 0.6 broadcast_multiply_fusion
  (8 shorter events, 0.2 us)
Async XLA Ops:
  4.5 4.7 %copy-start = (f32[48,256]{1,0:T(8,128)}, f32[48,256]{1,0:T(8,128)S(1)}, u32[]{:S(2)}) copy-start(f32[48,256]{1,0:T(8,128)S(1)} %get-tuple-element.7.mask_ref) | copy-start | bytes 147460
  4.5 4.4 %collective-permute-start = (f32[2,2,4,48,256]{4,3,2,1,0:T(8,128)S(1)}, f32[2,2,4,48,256]{4,3,2,1,0:T(8,128)S(1)}, u32[]{:S(2)}, u32[]{:S(2)}) collective-permute-start(f32[2,2,4,48,256]{4,3,2,1,0:T(8,128)S(1)} %slice_bitcast_fusion.2), channel_id=1, source_target_pairs={{0,1},{1,0},{2,3},{3,2},{4,5},{5,4},{6,7},{7,6},{8,9},{9,8},{10,11... | collective-permute-start | bytes 2359304 | tf_op jit(solution)/shard_map/ppermute | solution.py:131
  6.5 10.4 %collective-permute-start.3 = (f32[2,2,4,48,256]{4,3,2,0,1:T(8,128)S(1)}, f32[2,2,4,48,256]{4,3,2,0,1:T(8,128)S(1)}, u32[]{:S(2)}, u32[]{:S(2)}) collective-permute-start(f32[2,2,4,48,256]{4,3,2,0,1:T(8,128)S(1)} %slice_bitcast_fusion), channel_id=1, source_target_pairs={{0,1},{1,0},{2,3},{3,2},{4,5},{5,4},{6,7},{7,6},{8,9},{9,8},{10,11... | collective-permute-start | bytes 2359304 | tf_op jit(solution)/shard_map/ppermute | solution.py:132
  9.1 17.1 %collective-permute-start.1 = (f32[2,4,48,256]{3,2,1,0:T(8,128)S(1)}, f32[2,4,48,256]{3,2,1,0:T(8,128)S(1)}, u32[]{:S(2)}, u32[]{:S(2)}) collective-permute-start(f32[2,4,48,256]{3,2,1,0:T(8,128)S(1)} %slice_bitcast_fusion.5), channel_id=1, source_target_pairs={{0,2},{1,3},{2,0},{3,1},{4,6},{5,7},{6,4},{7,5},{8,10},{9,11},{10,... | collective-permute-start | bytes 1179656 | tf_op jit(solution)/shard_map/ppermute | solution.py:133
  17.1 12.6 %collective-permute-start.4 = (f32[2,4,48,256]{3,2,1,0:T(8,128)S(1)}, f32[2,4,48,256]{3,2,1,0:T(8,128)S(1)}, u32[]{:S(2)}, u32[]{:S(2)}) collective-permute-start(f32[2,4,48,256]{3,2,1,0:T(8,128)S(1)} %slice_bitcast_fusion.3), channel_id=1, source_target_pairs={{0,4},{1,5},{2,6},{3,7},{4,0},{5,1},{6,2},{7,3},{8,12},{9,13},{10,... | collective-permute-start | bytes 1179656 | tf_op jit(solution)/shard_map/ppermute | solution.py:134
  26.3 8.2 %collective-permute-start.2 = (f32[4,48,256]{2,1,0:T(8,128)S(1)}, f32[4,48,256]{2,1,0:T(8,128)S(1)}, u32[]{:S(2)}, u32[]{:S(2)}) collective-permute-start(f32[4,48,256]{2,1,0:T(8,128)S(1)} %slice_bitcast_fusion.9), channel_id=1, source_target_pairs={{0,4},{1,5},{2,6},{3,7},{4,0},{5,1},{6,2},{7,3},{8,12},{9,13},{10,... | collective-permute-start | bytes 589832 | tf_op jit(solution)/shard_map/ppermute | solution.py:135
  29.8 7.6 %collective-permute-start.5 = (f32[4,48,256]{2,1,0:T(8,128)S(1)}, f32[4,48,256]{2,1,0:T(8,128)S(1)}, u32[]{:S(2)}, u32[]{:S(2)}) collective-permute-start(f32[4,48,256]{2,1,0:T(8,128)S(1)} %slice_bitcast_fusion.7), channel_id=1, source_target_pairs={{0,2},{1,3},{2,0},{3,1},{4,6},{5,7},{6,4},{7,5},{8,10},{9,11},{10,... | collective-permute-start | bytes 589832 | tf_op jit(solution)/shard_map/ppermute | solution.py:136

commit v3 on v2

--- a/solution.py
+++ b/solution.py
@@ -32,10 +32,11 @@
     return (2 * pair + (group ^ (pair // 4))) * 4 + x * 2 + core
 
 
-def swapped(dgroup, dx, dcore):
+def partners(of):
     pairs = []
     for f in range(64):
         pair, group, x, core = place(f)
+        dgroup, dx, dcore = of(core)
         pairs.append((f, index_of(pair, group ^ dgroup, x ^ dx, core ^ dcore)))
     return pairs
 
@@ -45,7 +46,7 @@
 
 
 def partial_kernel(
-    acts_hbm, cot_hbm, chosen_hbm, out_ref, mask_ref, acts, cot, chosen_ref, acts_sem, cot_sem, chosen_sem
+    acts_hbm, cot_hbm, chosen_hbm, away_ref, near_ref, keep_away_ref, keep_near_ref, mask_ref, product, acts, cot, chosen_ref, acts_sem, cot_sem, chosen_sem
 ):
     copy_chosen = pltpu.make_async_copy(chosen_hbm, chosen_ref, chosen_sem)
     copy_chosen.start()
@@ -63,18 +64,25 @@
             hit = hit | (component == chosen_ref[c, j : j + 1, :])
         masks.append(jnp.where(hit, 1.0, 0.0))
     mask_ref[...] = jnp.concatenate(masks, axis=0).T
+    send_refs, keep_refs = (away_ref, near_ref), (keep_away_ref, keep_near_ref)
     _, group, x, core = place(lax.axis_index("fsdp"))
     copy_cot.wait()
     turned = cot[...].T
     copy_acts.wait()
     width = acts.shape[1] // 4
     for step in range(4):
-        product = jnp.dot(
+        product[...] = jnp.dot(
             turned, acts[:, step * width : (step + 1) * width], preferred_element_type=jnp.float32
         ).T
-        for at in range(0, width, rows):
-            pair, bit, to_x, to_core = place((step * width + at) // rows)
-            out_ref[to_core ^ core, pair // 4, to_x ^ x, bit ^ group, pair % 4] = product[at : at + rows]
+        for local in range(width // (8 * rows)):
+            pair = step * (width // (8 * rows)) + local
+            for slot in range(4):
+                early, late = 1 - slot // 2, 1 - slot % 2
+                for to_core, at_core in ((core, keep_refs), (1 - core, send_refs)):
+                    to_x = jnp.where(to_core == 0, early, late) ^ x
+                    bit = jnp.where(to_core == 0, late, early) ^ group ^ (pair // 4)
+                    at = (((local * 2 + bit) * 2 + to_x) * 2 + to_core) * rows
+                    at_core[slot // 2][slot % 2, pair] = product[pl.ds(pl.multiple_of(at, 8), rows)]
 
 
 def partials(acts, cot, chosen):
@@ -88,10 +96,14 @@
             pl.BlockSpec(memory_space=pl.ANY),
         ],
         out_shape=(
-            jax.ShapeDtypeStruct((2, 2, 2, 2, PAIRS // 2, dim // (8 * PAIRS), cols), jnp.float32),
+            jax.ShapeDtypeStruct((2, PAIRS, rows, cols), jnp.float32),
+            jax.ShapeDtypeStruct((2, PAIRS, rows, cols), jnp.float32),
+            jax.ShapeDtypeStruct((2, PAIRS, rows, cols), jnp.float32),
+            jax.ShapeDtypeStruct((2, PAIRS, rows, cols), jnp.float32),
             jax.ShapeDtypeStruct((rows, cols), jnp.float32),
         ),
         scratch_shapes=[
+            pltpu.VMEM((dim // 4, cols), jnp.float32),
             pltpu.VMEM(acts.shape, acts.dtype),
             pltpu.VMEM(cot.shape, cot.dtype),
             pltpu.VMEM(chosen.shape, chosen.dtype),
@@ -122,19 +134,36 @@
             jax.ShapeDtypeStruct((rows, cols), jnp.float32),
             jax.ShapeDtypeStruct((copies, rows, cols), jnp.float32),
         ),
+        compiler_params=pltpu.CompilerParams(vmem_limit_bytes=16 << 20),
     )(pieces, moment, mask, jnp.asarray(span_tables(cols)))
+
+
+def add_kernel(a_ref, b_ref, out_ref):
+    out_ref[...] = a_ref[...] + b_ref[...]
+
+
+def add(a, b):
+    return pl.pallas_call(
+        add_kernel,
+        out_shape=jax.ShapeDtypeStruct(a.shape, a.dtype),
+        compiler_params=pltpu.CompilerParams(vmem_limit_bytes=4 << 20),
+        cost_estimate=pl.CostEstimate(flops=a.size, bytes_accessed=3 * a.nbytes, transcendentals=0),
+    )(a, b)
 
 
 def shards(activations, cotangent, momentum, components):
     groups = lax.axis_size("rep")
-    part, mask = partials(activations[0], cotangent[0], components[0].transpose(1, 2, 0))
-    first = part[0, 0] + lax.ppermute(part[1, 0], "fsdp", swapped(0, 0, 1))
-    second = part[0, 1] + lax.ppermute(part[1, 1], "fsdp", swapped(0, 0, 1))
-    first = first[0] + lax.ppermute(first[1], "fsdp", swapped(0, 1, 0))
-    second = second[:, 0] + lax.ppermute(second[:, 1], "fsdp", swapped(1, 0, 0))
-    first = first[0] + lax.ppermute(first[1], "fsdp", swapped(1, 0, 0))
-    second = second[0] + lax.ppermute(second[1], "fsdp", swapped(0, 1, 0))
-    mine = jnp.concatenate([first, second])
+    away, near, kept_away, kept_near, mask = partials(
+        activations[0], cotangent[0], components[0].transpose(1, 2, 0)
+    )
+    core = partners(lambda core: (0, 0, 1))
+    once, twice = partners(lambda core: (core, 1 - core, 0)), partners(lambda core: (1 - core, core, 0))
+    away = lax.ppermute(away, "fsdp", core)
+    near = add(kept_near, lax.ppermute(near, "fsdp", core))
+    two = lax.ppermute(kept_away[0] + away[0], "fsdp", once)
+    one = lax.ppermute(kept_away[1] + away[1], "fsdp", once)
+    here = add(near[1], one)
+    mine = here + lax.ppermute(near[0] + two, "fsdp", twice)
     members = [
         [index_of(pair, group, x, core) for pair in range(PAIRS)]
         for group in range(2)

time: 90.5 us -> 85.6 us (0.946)
  the two profiles are of different devices: /device:TPU:2 before, /device:TPU:32 now
where the time goes in v3:
time: 85.6 us; the launch traced here: 85.2 us
  blocking collectives  51 us (60%)
  starting transfers between devices  17.7 us (21%)
  waiting for transfers between devices  9.36 us (11%)
  Pallas kernels  5.44 us (6%)
  other arithmetic  0.86 us (1%)
    all_to_all x1, blocking collectives, shards(): pieces = lax.all_to_all(mine, 'fsdp', 0, 0, axis_index_groups=members)  34.7 us
    all_to_all x1, blocking collectives, shards(): restored = lax.all_to_all(copies, 'rep', 0, 0)  16.3 us
    ppermute x1, starting transfers between devices, shards(): mine = here + lax.ppermute(near[0] + two, 'fsdp', twice)  7.39 us
    ppermute x1, waiting for transfers between devices, shards(): mine = here + lax.ppermute(near[0] + two, 'fsdp', twice)  5.64 us
    pallas_call x1, Pallas kernels, partials(): pl.pallas_call(partial_kernel, in_specs=[pl.BlockSpec(memory_space=pl.ANY...  3.93 us
    ppermute x1, waiting for transfers between devices, shards(): two = lax.ppermute(kept_away[0] + away[0], 'fsdp', once)  3.71 us
    ppermute x1, starting transfers between devices, shards(): two = lax.ppermute(kept_away[0] + away[0], 'fsdp', once)  3.53 us
    ppermute x1, starting transfers between devices, shards(): one = lax.ppermute(kept_away[1] + away[1], 'fsdp', once)  2.45 us
  transfers between devices with their start and end apart: 5, of which 2 were waited for; matrix products, arithmetic and copies ran while one was open for 0% of the time, Pallas kernels for 0%

profile of v3, /device:TPU:32, one launch (start us, length us, event | category | flops | bytes accessed | tf_op | source)
XLA Modules:
  0.0 85.2 jit_solution(5026400089582569991)
XLA Ops:
  0.6 3.9 %shard_map.68 = (f32[2,8,48,256]{3,2,1,0:T(8,128)S(1)}, f32[2,8,48,256]{3,2,1,0:T(8,128)S(1)}, f32[2,8,48,256]{3,2,1,0:T(8,128)S(1)}, f32[2,8,48,256]{3,2,1,0:T(8,128)S(1)}, f32[48,256]{1,0:T(8,128)S(1)}) custom-call(bf16[640,3072]{1,0:T(8,128)(2,1)} %bitcast.18, bf16[640,256]{1,0:T(8,128)(2,1)} %bitcast.19, s32[4,8,48]{2,1,0:T(8,128)} %bitcast.20), custom_call_target="tpu_custom_call" | custom-call | tf_op jit(solution)/shard_map/pallas_call | solution.py:91
  4.6 1.9 %collective-permute-start.1 = (f32[2,8,48,256]{3,2,1,0:T(8,128)S(1)}, f32[2,8,48,256]{3,2,1,0:T(8,128)S(1)}, u32[]{:S(2)}, u32[]{:S(2)}) collective-permute-start(f32[2,8,48,256]{3,2,1,0:T(8,128)S(1)} %get-tuple-element.12), channel_id=1, source_target_pairs={{0,1},{1,0},{2,3},{3,2},{4,5},{5,4},{6,7},{7,6},{8,9},{9,8},{10,11... | collective-permute-start | bytes 2359304 | tf_op jit(solution)/shard_map/ppermute | solution.py:161
  6.5 2.4 %collective-permute-start = (f32[2,8,48,256]{3,2,1,0:T(8,128)S(1)}, f32[2,8,48,256]{3,2,1,0:T(8,128)S(1)}, u32[]{:S(2)}, u32[]{:S(2)}) collective-permute-start(f32[2,8,48,256]{3,2,1,0:T(8,128)S(1)} %get-tuple-element.10), channel_id=1, source_target_pairs={{0,1},{1,0},{2,3},{3,2},{4,5},{5,4},{6,7},{7,6},{8,9},{9,8},{10,11... | collective-permute-start | bytes 2359304 | tf_op jit(solution)/shard_map/ppermute | solution.py:162
  8.9 0.0 collective-permute-done.1
  8.9 0.1 fusion
  9.0 0.0 copy-start
  9.0 0.0 copy-start.1
  9.1 3.5 %collective-permute-start.3 = (f32[8,48,256]{2,1,0:T(8,128)S(1)}, f32[8,48,256]{2,1,0:T(8,128)S(1)}, u32[]{:S(2)}, u32[]{:S(2)}) collective-permute-start(f32[8,48,256]{2,1,0:T(8,128)S(1)} %get-tuple-element.16), channel_id=1, source_target_pairs={{0,2},{1,5},{2,0},{3,7},{4,6},{5,1},{6,4},{7,3},{8,10},{9,13},{10,... | collective-permute-start | bytes 1179656 | tf_op jit(solution)/shard_map/ppermute | solution.py:163
  12.6 2.4 %collective-permute-start.2 = (f32[8,48,256]{2,1,0:T(8,128)S(1)}, f32[8,48,256]{2,1,0:T(8,128)S(1)}, u32[]{:S(2)}, u32[]{:S(2)}) collective-permute-start(f32[8,48,256]{2,1,0:T(8,128)S(1)} %get-tuple-element.17), channel_id=1, source_target_pairs={{0,2},{1,5},{2,0},{3,7},{4,6},{5,1},{6,4},{7,3},{8,10},{9,13},{10,... | collective-permute-start | bytes 1179656 | tf_op jit(solution)/shard_map/ppermute | solution.py:164
  15.0 0.0 collective-permute-done.b_ref
  15.1 0.1 shard_map.69
  15.1 3.7 %collective-permute-done.3 = f32[8,48,256]{2,1,0:T(8,128)S(1)} collective-permute-done((f32[8,48,256]{2,1,0:T(8,128)S(1)}, f32[8,48,256]{2,1,0:T(8,128)S(1)}, u32[]{:S(2)}, u32[]{:S(2)}) %collective-permute-start.3) | collective-permute-done | bytes 393248 | tf_op jit(solution)/shard_map/ppermute | solution.py:163
  18.9 0.1 fusion.1
  18.9 7.4 %collective-permute-start.4 = (f32[8,48,256]{2,1,0:T(8,128)S(1)}, f32[8,48,256]{2,1,0:T(8,128)S(1)}, u32[]{:S(2)}, u32[]{:S(2)}) collective-permute-start(f32[8,48,256]{2,1,0:T(8,128)S(1)} %fusion.1), channel_id=1, source_target_pairs={{0,4},{1,3},{2,6},{3,1},{4,0},{5,7},{6,2},{7,5},{8,12},{9,11},{10,... | collective-permute-start | bytes 1179656 | tf_op jit(solution)/shard_map/ppermute | solution.py:166
  26.4 0.0 collective-permute-done.2.b_ref
  26.4 5.6 %collective-permute-done.4 = f32[8,48,256]{2,1,0:T(8,128)S(1)} collective-permute-done((f32[8,48,256]{2,1,0:T(8,128)S(1)}, f32[8,48,256]{2,1,0:T(8,128)S(1)}, u32[]{:S(2)}, u32[]{:S(2)}) %collective-permute-start.4) | collective-permute-done | bytes 393248 | tf_op jit(solution)/shard_map/ppermute | solution.py:166
  32.1 0.1 add.23
  32.1 34.7 %all_to_all.10.pieces_ref = f32[8,48,256]{2,1,0:T(8,128)S(1)} all-to-all(f32[8,48,256]{2,1,0:T(8,128)S(1)} %add.23), channel_id=1, replica_groups={{0,8,16,24,36,44,52,60},{1,9,17,25,37,45,53,61},{2,10,18,26,38,46,54,62..., dimensions={0} | all-to-all | bytes 786432 | tf_op jit(solution)/shard_map/all_to_all | solution.py:173
  66.8 0.0 copy-done
  66.8 0.0 copy-done.1
  66.8 1.4 %shard_map.71 = (f32[48,256]{1,0:T(8,128)}, f32[8,48,256]{2,1,0:T(8,128)S(1)}) custom-call(f32[8,48,256]{2,1,0:T(8,128)S(1)} %all_to_all.10.pieces_ref, f32[48,256]{1,0:T(8,128)S(1)} %bitcast.17, f32[48,256]{1,0:T(8,128)S(1)} %get-tuple-element.13.mask_ref, f32[256,256]{1,0:T(8,128)S(1)} %copy-done), custom_call_target="tpu_custom_call" | custom-call | tf_op jit(solution)/shard_map/pallas_call | solution.py:131
  68.2 16.3 %all_to_all.11 = f32[8,48,256]{2,1,0:T(8,128)S(1)} all-to-all(f32[8,48,256]{2,1,0:T(8,128)S(1)} %get-tuple-element.14), channel_id=1, replica_groups=mesh['rep'=8,'fsdp'=64] {'rep'}, dimensions={0} | all-to-all | bytes 786432 | tf_op jit(solution)/shard_map/all_to_all | solution.py:175
  84.6 0.6 broadcast_multiply_fusion
  (3 shorter events, 0.1 us)
Async XLA Ops:
  4.6 4.3 %collective-permute-start.1 = (f32[2,8,48,256]{3,2,1,0:T(8,128)S(1)}, f32[2,8,48,256]{3,2,1,0:T(8,128)S(1)}, u32[]{:S(2)}, u32[]{:S(2)}) collective-permute-start(f32[2,8,48,256]{3,2,1,0:T(8,128)S(1)} %get-tuple-element.12), channel_id=1, source_target_pairs={{0,1},{1,0},{2,3},{3,2},{4,5},{5,4},{6,7},{7,6},{8,9},{9,8},{10,11... | collective-permute-start | bytes 2359304 | tf_op jit(solution)/shard_map/ppermute | solution.py:161
  6.5 8.6 %collective-permute-start = (f32[2,8,48,256]{3,2,1,0:T(8,128)S(1)}, f32[2,8,48,256]{3,2,1,0:T(8,128)S(1)}, u32[]{:S(2)}, u32[]{:S(2)}) collective-permute-start(f32[2,8,48,256]{3,2,1,0:T(8,128)S(1)} %get-tuple-element.10), channel_id=1, source_target_pairs={{0,1},{1,0},{2,3},{3,2},{4,5},{5,4},{6,7},{7,6},{8,9},{9,8},{10,11... | collective-permute-start | bytes 2359304 | tf_op jit(solution)/shard_map/ppermute | solution.py:162
  9.0 57.8 %copy-start = (f32[256,256]{1,0:T(8,128)S(1)}, f32[256,256]{1,0:T(8,128)}, u32[]{:S(2)}) copy-start(f32[256,256]{1,0:T(8,128)} %constant.7.clone.table_ref) | copy-start | bytes 786436
  9.0 57.8 %copy-start.1 = (f32[1,48,256]{2,1,0:T(8,128)S(1)}, f32[1,48,256]{2,1,0:T(8,128)}, u32[]{:S(2)}) copy-start(f32[1,48,256]{2,1,0:T(8,128)} %param.7) | copy-start | bytes 147460
  9.1 9.8 %collective-permute-start.3 = (f32[8,48,256]{2,1,0:T(8,128)S(1)}, f32[8,48,256]{2,1,0:T(8,128)S(1)}, u32[]{:S(2)}, u32[]{:S(2)}) collective-permute-start(f32[8,48,256]{2,1,0:T(8,128)S(1)} %get-tuple-element.16), channel_id=1, source_target_pairs={{0,2},{1,5},{2,0},{3,7},{4,6},{5,1},{6,4},{7,3},{8,10},{9,13},{10,... | collective-permute-start | bytes 1179656 | tf_op jit(solution)/shard_map/ppermute | solution.py:163
  12.6 13.8 %collective-permute-start.2 = (f32[8,48,256]{2,1,0:T(8,128)S(1)}, f32[8,48,256]{2,1,0:T(8,128)S(1)}, u32[]{:S(2)}, u32[]{:S(2)}) collective-permute-start(f32[8,48,256]{2,1,0:T(8,128)S(1)} %get-tuple-element.17), channel_id=1, source_target_pairs={{0,2},{1,5},{2,0},{3,7},{4,6},{5,1},{6,4},{7,3},{8,10},{9,13},{10,... | collective-permute-start | bytes 1179656 | tf_op jit(solution)/shard_map/ppermute | solution.py:164
  18.9 13.1 %collective-permute-start.4 = (f32[8,48,256]{2,1,0:T(8,128)S(1)}, f32[8,48,256]{2,1,0:T(8,128)S(1)}, u32[]{:S(2)}, u32[]{:S(2)}) collective-permute-start(f32[8,48,256]{2,1,0:T(8,128)S(1)} %fusion.1), channel_id=1, source_target_pairs={{0,4},{1,3},{2,6},{3,1},{4,0},{5,7},{6,2},{7,5},{8,12},{9,11},{10,... | collective-permute-start | bytes 1179656 | tf_op jit(solution)/shard_map/ppermute | solution.py:166

commit v4 on v3

--- a/solution.py
+++ b/solution.py
@@ -11,7 +11,6 @@
 SPAN = 64
 PAIRS = 8
 beta_decay = 0.999
-highest = lax.Precision.HIGHEST
 
 
 def span_tables(cols):
@@ -22,14 +21,19 @@
     return np.kron(np.eye(cols // SPAN), cosines.T).astype(np.float32)
 
 
+def two_parts(table):
+    high = table.astype(jnp.bfloat16)
+    return np.stack([high, (table - high.astype(np.float32)).astype(jnp.bfloat16)])
+
+
 def place(index):
     z = index // 4
     pair, bit = z // 2, z % 2
-    return pair, bit ^ (pair // 4), (index // 2) % 2, index % 2
+    return pair, bit ^ ((60 >> pair) & 1), (index // 2) % 2, index % 2
 
 
 def index_of(pair, group, x, core):
-    return (2 * pair + (group ^ (pair // 4))) * 4 + x * 2 + core
+    return (2 * pair + (group ^ ((60 >> pair) & 1))) * 4 + x * 2 + core
 
 
 def partners(of):
@@ -52,8 +56,13 @@
     copy_chosen.start()
     copy_cot = pltpu.make_async_copy(cot_hbm, cot, cot_sem)
     copy_cot.start()
-    copy_acts = pltpu.make_async_copy(acts_hbm, acts, acts_sem)
-    copy_acts.start()
+    half = acts.shape[1] // 2
+    copies = [
+        pltpu.make_async_copy(acts_hbm.at[:, pl.ds(at, half)], acts.at[:, pl.ds(at, half)], acts_sem.at[at // half])
+        for at in (0, half)
+    ]
+    for copy in copies:
+        copy.start()
     spans, kept, rows = chosen_ref.shape
     copy_chosen.wait()
     component = lax.broadcasted_iota(jnp.int32, (SPAN, rows), 0)
@@ -68,9 +77,10 @@
     _, group, x, core = place(lax.axis_index("fsdp"))
     copy_cot.wait()
     turned = cot[...].T
-    copy_acts.wait()
     width = acts.shape[1] // 4
     for step in range(4):
+        if step % 2 == 0:
+            copies[step // 2].wait()
         product[...] = jnp.dot(
             turned, acts[:, step * width : (step + 1) * width], preferred_element_type=jnp.float32
         ).T
@@ -80,7 +90,7 @@
                 early, late = 1 - slot // 2, 1 - slot % 2
                 for to_core, at_core in ((core, keep_refs), (1 - core, send_refs)):
                     to_x = jnp.where(to_core == 0, early, late) ^ x
-                    bit = jnp.where(to_core == 0, late, early) ^ group ^ (pair // 4)
+                    bit = jnp.where(to_core == 0, late, early) ^ group ^ ((60 >> pair) & 1)
                     at = (((local * 2 + bit) * 2 + to_x) * 2 + to_core) * rows
                     at_core[slot // 2][slot % 2, pair] = product[pl.ds(pl.multiple_of(at, 8), rows)]
 
@@ -107,7 +117,7 @@
             pltpu.VMEM(acts.shape, acts.dtype),
             pltpu.VMEM(cot.shape, cot.dtype),
             pltpu.VMEM(chosen.shape, chosen.dtype),
-            pltpu.SemaphoreType.DMA,
+            pltpu.SemaphoreType.DMA((2,)),
             pltpu.SemaphoreType.DMA,
             pltpu.SemaphoreType.DMA,
         ],
@@ -115,13 +125,27 @@
     )(in_hbm(acts), in_hbm(cot), in_hbm(chosen))
 
 
+def split(array):
+    high = array.astype(jnp.bfloat16)
+    return high, (array - high.astype(jnp.float32)).astype(jnp.bfloat16)
+
+
+def product(array, table_ref, contract):
+    high, low = split(array)
+    rows = array.shape[0]
+    dims = (((1,), (contract,)), ((), ()))
+    both = lax.dot_general(
+        jnp.concatenate([high, low]), table_ref[0], dims, preferred_element_type=jnp.float32
+    )
+    rest = lax.dot_general(high, table_ref[1], dims, preferred_element_type=jnp.float32)
+    return both[:rows] + (both[rows:] + rest)
+
+
 def encode_kernel(pieces_ref, moment_ref, mask_ref, table_ref, renewed_ref, copies_ref):
     moment_new = beta_decay * moment_ref[...] + jnp.sum(pieces_ref[...], axis=0)
-    spectrum = jnp.dot(moment_new, table_ref[...], precision=highest, preferred_element_type=jnp.float32)
+    spectrum = product(moment_new, table_ref, 0)
     retained = jnp.where(mask_ref[...] > 0.5, spectrum, 0.0)
-    restored = lax.dot_general(
-        retained, table_ref[...], (((1,), (1,)), ((), ())), precision=highest, preferred_element_type=jnp.float32
-    )
+    restored = product(retained, table_ref, 1)
     renewed_ref[...] = moment_new - restored
     copies_ref[...] = jnp.broadcast_to(restored, copies_ref.shape)
 
@@ -135,7 +159,7 @@
             jax.ShapeDtypeStruct((copies, rows, cols), jnp.float32),
         ),
         compiler_params=pltpu.CompilerParams(vmem_limit_bytes=16 << 20),
-    )(pieces, moment, mask, jnp.asarray(span_tables(cols)))
+    )(pieces, moment, mask, jnp.asarray(two_parts(span_tables(cols))))
 
 
 def add_kernel(a_ref, b_ref, out_ref):

time: 85.6 us -> 84.9 us (level)
  no operation moved by 1% of the time
where the time goes in v4:
time: 84.9 us; the launch traced here: 84.6 us
  blocking collectives  51 us (60%)
  starting transfers between devices  17.7 us (21%)
  waiting for transfers between devices  9.36 us (11%)
  Pallas kernels  4.92 us (6%)
  other arithmetic  0.86 us (1%)
    all_to_all x1, blocking collectives, shards(): pieces = lax.all_to_all(mine, 'fsdp', 0, 0, axis_index_groups=members)  34.6 us
    all_to_all x1, blocking collectives, shards(): restored = lax.all_to_all(copies, 'rep', 0, 0)  16.3 us
    ppermute x1, starting transfers between devices, shards(): mine = here + lax.ppermute(near[0] + two, 'fsdp', twice)  7.39 us
    ppermute x1, waiting for transfers between devices, shards(): mine = here + lax.ppermute(near[0] + two, 'fsdp', twice)  5.64 us
    pallas_call x1, Pallas kernels, partials(): pl.pallas_call(partial_kernel, in_specs=[pl.BlockSpec(memory_space=pl.ANY...  3.79 us
    ppermute x1, waiting for transfers between devices, shards(): two = lax.ppermute(kept_away[0] + away[0], 'fsdp', once)  3.71 us
    ppermute x1, starting transfers between devices, shards(): two = lax.ppermute(kept_away[0] + away[0], 'fsdp', once)  3.53 us
    ppermute x1, starting transfers between devices, shards(): one = lax.ppermute(kept_away[1] + away[1], 'fsdp', once)  2.44 us
  transfers between devices with their start and end apart: 5, of which 2 were waited for; matrix products, arithmetic and copies ran while one was open for 0% of the time, Pallas kernels for 0%

profile of v4, /device:TPU:32, one launch (start us, length us, event | category | flops | bytes accessed | tf_op | source)
XLA Modules:
  0.0 84.6 jit_solution(9835237999324014008)
XLA Ops:
  0.6 3.8 %shard_map.68 = (f32[2,8,48,256]{3,2,1,0:T(8,128)S(1)}, f32[2,8,48,256]{3,2,1,0:T(8,128)S(1)}, f32[2,8,48,256]{3,2,1,0:T(8,128)S(1)}, f32[2,8,48,256]{3,2,1,0:T(8,128)S(1)}, f32[48,256]{1,0:T(8,128)S(1)}) custom-call(bf16[640,3072]{1,0:T(8,128)(2,1)} %bitcast.18, bf16[640,256]{1,0:T(8,128)(2,1)} %bitcast.19, s32[4,8,48]{2,1,0:T(8,128)} %bitcast.20), custom_call_target="tpu_custom_call" | custom-call | tf_op jit(solution)/shard_map/pallas_call | solution.py:101
  4.4 1.9 %collective-permute-start.1 = (f32[2,8,48,256]{3,2,1,0:T(8,128)S(1)}, f32[2,8,48,256]{3,2,1,0:T(8,128)S(1)}, u32[]{:S(2)}, u32[]{:S(2)}) collective-permute-start(f32[2,8,48,256]{3,2,1,0:T(8,128)S(1)} %get-tuple-element.12), channel_id=1, source_target_pairs={{0,1},{1,0},{2,3},{3,2},{4,5},{5,4},{6,7},{7,6},{8,9},{9,8},{10,11... | collective-permute-start | bytes 2359304 | tf_op jit(solution)/shard_map/ppermute | solution.py:185
  6.4 2.4 %collective-permute-start = (f32[2,8,48,256]{3,2,1,0:T(8,128)S(1)}, f32[2,8,48,256]{3,2,1,0:T(8,128)S(1)}, u32[]{:S(2)}, u32[]{:S(2)}) collective-permute-start(f32[2,8,48,256]{3,2,1,0:T(8,128)S(1)} %get-tuple-element.10), channel_id=1, source_target_pairs={{0,1},{1,0},{2,3},{3,2},{4,5},{5,4},{6,7},{7,6},{8,9},{9,8},{10,11... | collective-permute-start | bytes 2359304 | tf_op jit(solution)/shard_map/ppermute | solution.py:186
  8.8 0.0 collective-permute-done.1
  8.8 0.1 fusion
  8.9 0.0 copy-start
  8.9 0.0 copy-start.1
  8.9 3.5 %collective-permute-start.3 = (f32[8,48,256]{2,1,0:T(8,128)S(1)}, f32[8,48,256]{2,1,0:T(8,128)S(1)}, u32[]{:S(2)}, u32[]{:S(2)}) collective-permute-start(f32[8,48,256]{2,1,0:T(8,128)S(1)} %get-tuple-element.16), channel_id=1, source_target_pairs={{0,2},{1,5},{2,0},{3,7},{4,6},{5,1},{6,4},{7,3},{8,10},{9,13},{10,... | collective-permute-start | bytes 1179656 | tf_op jit(solution)/shard_map/ppermute | solution.py:187
  12.5 2.4 %collective-permute-start.2 = (f32[8,48,256]{2,1,0:T(8,128)S(1)}, f32[8,48,256]{2,1,0:T(8,128)S(1)}, u32[]{:S(2)}, u32[]{:S(2)}) collective-permute-start(f32[8,48,256]{2,1,0:T(8,128)S(1)} %get-tuple-element.17), channel_id=1, source_target_pairs={{0,2},{1,5},{2,0},{3,7},{4,6},{5,1},{6,4},{7,3},{8,10},{9,13},{10,... | collective-permute-start | bytes 1179656 | tf_op jit(solution)/shard_map/ppermute | solution.py:188
  14.9 0.0 collective-permute-done.b_ref
  14.9 0.1 shard_map.69
  15.0 3.7 %collective-permute-done.3 = f32[8,48,256]{2,1,0:T(8,128)S(1)} collective-permute-done((f32[8,48,256]{2,1,0:T(8,128)S(1)}, f32[8,48,256]{2,1,0:T(8,128)S(1)}, u32[]{:S(2)}, u32[]{:S(2)}) %collective-permute-start.3) | collective-permute-done | bytes 393248 | tf_op jit(solution)/shard_map/ppermute | solution.py:187
  18.7 0.1 fusion.1
  18.8 7.4 %collective-permute-start.4 = (f32[8,48,256]{2,1,0:T(8,128)S(1)}, f32[8,48,256]{2,1,0:T(8,128)S(1)}, u32[]{:S(2)}, u32[]{:S(2)}) collective-permute-start(f32[8,48,256]{2,1,0:T(8,128)S(1)} %fusion.1), channel_id=1, source_target_pairs={{0,4},{1,3},{2,6},{3,1},{4,0},{5,7},{6,2},{7,5},{8,12},{9,11},{10,... | collective-permute-start | bytes 1179656 | tf_op jit(solution)/shard_map/ppermute | solution.py:190
  26.2 0.0 collective-permute-done.2.b_ref
  26.3 5.6 %collective-permute-done.4 = f32[8,48,256]{2,1,0:T(8,128)S(1)} collective-permute-done((f32[8,48,256]{2,1,0:T(8,128)S(1)}, f32[8,48,256]{2,1,0:T(8,128)S(1)}, u32[]{:S(2)}, u32[]{:S(2)}) %collective-permute-start.4) | collective-permute-done | bytes 393248 | tf_op jit(solution)/shard_map/ppermute | solution.py:190
  31.9 0.1 add.23
  32.0 34.6 %all_to_all.10.pieces_ref = f32[8,48,256]{2,1,0:T(8,128)S(1)} all-to-all(f32[8,48,256]{2,1,0:T(8,128)S(1)} %add.23), channel_id=1, replica_groups={{0,8,20,28,36,44,48,56},{1,9,21,29,37,45,49,57},{2,10,22,30,38,46,50,58..., dimensions={0} | all-to-all | bytes 786432 | tf_op jit(solution)/shard_map/all_to_all | solution.py:197
  66.6 0.0 copy-done
  66.6 0.0 copy-done.1
  66.6 1.0 %shard_map.71 = (f32[48,256]{1,0:T(8,128)}, f32[8,48,256]{2,1,0:T(8,128)S(1)}) custom-call(f32[8,48,256]{2,1,0:T(8,128)S(1)} %all_to_all.10.pieces_ref, f32[48,256]{1,0:T(8,128)S(1)} %bitcast.17, f32[48,256]{1,0:T(8,128)S(1)} %get-tuple-element.13.mask_ref, bf16[2,256,256]{2,1,0:T(8,128)(2,1)S(1)} %copy-done), custom_call_target="tpu_custom_call" | custom-call | tf_op jit(solution)/shard_map/pallas_call | solution.py:155
  67.6 16.3 %all_to_all.11 = f32[8,48,256]{2,1,0:T(8,128)S(1)} all-to-all(f32[8,48,256]{2,1,0:T(8,128)S(1)} %get-tuple-element.14), channel_id=1, replica_groups=mesh['rep'=8,'fsdp'=64] {'rep'}, dimensions={0} | all-to-all | bytes 786432 | tf_op jit(solution)/shard_map/all_to_all | solution.py:199
  84.0 0.6 broadcast_multiply_fusion
  (3 shorter events, 0.1 us)
Async XLA Ops:
  4.4 4.3 %collective-permute-start.1 = (f32[2,8,48,256]{3,2,1,0:T(8,128)S(1)}, f32[2,8,48,256]{3,2,1,0:T(8,128)S(1)}, u32[]{:S(2)}, u32[]{:S(2)}) collective-permute-start(f32[2,8,48,256]{3,2,1,0:T(8,128)S(1)} %get-tuple-element.12), channel_id=1, source_target_pairs={{0,1},{1,0},{2,3},{3,2},{4,5},{5,4},{6,7},{7,6},{8,9},{9,8},{10,11... | collective-permute-start | bytes 2359304 | tf_op jit(solution)/shard_map/ppermute | solution.py:185
  6.4 8.6 %collective-permute-start = (f32[2,8,48,256]{3,2,1,0:T(8,128)S(1)}, f32[2,8,48,256]{3,2,1,0:T(8,128)S(1)}, u32[]{:S(2)}, u32[]{:S(2)}) collective-permute-start(f32[2,8,48,256]{3,2,1,0:T(8,128)S(1)} %get-tuple-element.10), channel_id=1, source_target_pairs={{0,1},{1,0},{2,3},{3,2},{4,5},{5,4},{6,7},{7,6},{8,9},{9,8},{10,11... | collective-permute-start | bytes 2359304 | tf_op jit(solution)/shard_map/ppermute | solution.py:186
  8.9 57.7 %copy-start = (bf16[2,256,256]{2,1,0:T(8,128)(2,1)S(1)}, bf16[2,256,256]{2,1,0:T(8,128)(2,1)}, u32[]{:S(2)}) copy-start(bf16[2,256,256]{2,1,0:T(8,128)(2,1)} %constant.7.clone.table_ref) | copy-start | bytes 786436
  8.9 57.7 %copy-start.1 = (f32[1,48,256]{2,1,0:T(8,128)S(1)}, f32[1,48,256]{2,1,0:T(8,128)}, u32[]{:S(2)}) copy-start(f32[1,48,256]{2,1,0:T(8,128)} %param.7) | copy-start | bytes 147460
  8.9 9.8 %collective-permute-start.3 = (f32[8,48,256]{2,1,0:T(8,128)S(1)}, f32[8,48,256]{2,1,0:T(8,128)S(1)}, u32[]{:S(2)}, u32[]{:S(2)}) collective-permute-start(f32[8,48,256]{2,1,0:T(8,128)S(1)} %get-tuple-element.16), channel_id=1, source_target_pairs={{0,2},{1,5},{2,0},{3,7},{4,6},{5,1},{6,4},{7,3},{8,10},{9,13},{10,... | collective-permute-start | bytes 1179656 | tf_op jit(solution)/shard_map/ppermute | solution.py:187
  12.5 13.8 %collective-permute-start.2 = (f32[8,48,256]{2,1,0:T(8,128)S(1)}, f32[8,48,256]{2,1,0:T(8,128)S(1)}, u32[]{:S(2)}, u32[]{:S(2)}) collective-permute-start(f32[8,48,256]{2,1,0:T(8,128)S(1)} %get-tuple-element.17), channel_id=1, source_target_pairs={{0,2},{1,5},{2,0},{3,7},{4,6},{5,1},{6,4},{7,3},{8,10},{9,13},{10,... | collective-permute-start | bytes 1179656 | tf_op jit(solution)/shard_map/ppermute | solution.py:188
  18.8 13.1 %collective-permute-start.4 = (f32[8,48,256]{2,1,0:T(8,128)S(1)}, f32[8,48,256]{2,1,0:T(8,128)S(1)}, u32[]{:S(2)}, u32[]{:S(2)}) collective-permute-start(f32[8,48,256]{2,1,0:T(8,128)S(1)} %fusion.1), channel_id=1, source_target_pairs={{0,4},{1,3},{2,6},{3,1},{4,0},{5,7},{6,2},{7,5},{8,12},{9,11},{10,... | collective-permute-start | bytes 1179656 | tf_op jit(solution)/shard_map/ppermute | solution.py:190

commit v5 on v4

--- a/solution.py
+++ b/solution.py
@@ -9,7 +9,7 @@
 from jax.sharding import PartitionSpec as P
 
 SPAN = 64
-PAIRS = 8
+PAIRS = 4
 beta_decay = 0.999
 
 
@@ -28,21 +28,28 @@
 
 def place(index):
     z = index // 4
-    pair, bit = z // 2, z % 2
-    return pair, bit ^ ((60 >> pair) & 1), (index // 2) % 2, index % 2
-
-
-def index_of(pair, group, x, core):
-    return (2 * pair + (group ^ ((60 >> pair) & 1))) * 4 + x * 2 + core
-
-
-def partners(of):
-    pairs = []
-    for f in range(64):
-        pair, group, x, core = place(f)
-        dgroup, dx, dcore = of(core)
-        pairs.append((f, index_of(pair, group ^ dgroup, x ^ dx, core ^ dcore)))
-    return pairs
+    kind = ((z + 1) // 2) % 2
+    pair = ((z + 16 - 3 + 2 * kind) % 16) // 4
+    return pair, (1 - z % 2) ^ (pair // 2), kind, (index // 2) % 2, index % 2
+
+
+def index_of(pair, side, kind, x, core):
+    return ((4 * pair + 3 - 2 * kind + (side ^ (pair // 2))) % 16) * 4 + x * 2 + core
+
+
+def neighbour(index, way):
+    z, low = index // 4, index % 4
+    if way == "core":
+        return z * 4 + (low ^ 1)
+    if way == "x":
+        return z * 4 + (low ^ 2)
+    if way == "across":
+        return (z ^ 1) * 4 + low
+    return ((z + 2 * (z % 2) + 15) % 16) * 4 + low
+
+
+def partners(core_0, core_1):
+    return [(f, neighbour(f, core_1 if f % 2 else core_0)) for f in range(64)]
 
 
 def in_hbm(array):
@@ -73,26 +80,28 @@
             hit = hit | (component == chosen_ref[c, j : j + 1, :])
         masks.append(jnp.where(hit, 1.0, 0.0))
     mask_ref[...] = jnp.concatenate(masks, axis=0).T
-    send_refs, keep_refs = (away_ref, near_ref), (keep_away_ref, keep_near_ref)
-    _, group, x, core = place(lax.axis_index("fsdp"))
+    me = lax.axis_index("fsdp")
+    _, side, kind, x, core = place(me)
+    _, side_across, _, _, _ = place((me // 4 ^ 1) * 4)
     copy_cot.wait()
     turned = cot[...].T
     width = acts.shape[1] // 4
     for step in range(4):
         if step % 2 == 0:
             copies[step // 2].wait()
-        product[...] = jnp.dot(
+        product[step * width : (step + 1) * width] = jnp.dot(
             turned, acts[:, step * width : (step + 1) * width], preferred_element_type=jnp.float32
         ).T
-        for local in range(width // (8 * rows)):
-            pair = step * (width // (8 * rows)) + local
-            for slot in range(4):
-                early, late = 1 - slot // 2, 1 - slot % 2
-                for to_core, at_core in ((core, keep_refs), (1 - core, send_refs)):
-                    to_x = jnp.where(to_core == 0, early, late) ^ x
-                    bit = jnp.where(to_core == 0, late, early) ^ group ^ ((60 >> pair) & 1)
-                    at = (((local * 2 + bit) * 2 + to_x) * 2 + to_core) * rows
-                    at_core[slot // 2][slot % 2, pair] = product[pl.ds(pl.multiple_of(at, 8), rows)]
+    for slot in range(8):
+        first, second, third = 1 - slot // 4, 1 - slot // 2 % 2, 1 - slot % 2
+        for to_core, refs in ((core, (keep_away_ref, keep_near_ref)), (1 - core, (away_ref, near_ref))):
+            to_x = jnp.where(to_core == 0, first, third) ^ x
+            across = jnp.where(to_core == 0, second, first)
+            along = jnp.where(to_core == 0, third, second)
+            to_side = along ^ jnp.where(across == 1, side_across, side)
+            for pair in range(4):
+                at = index_of(pair, to_side, kind ^ across, to_x, to_core) * rows
+                refs[slot // 4][slot % 4, pair] = product[pl.ds(pl.multiple_of(at, 8), rows)]
 
 
 def partials(acts, cot, chosen):
@@ -106,14 +115,14 @@
             pl.BlockSpec(memory_space=pl.ANY),
         ],
         out_shape=(
-            jax.ShapeDtypeStruct((2, PAIRS, rows, cols), jnp.float32),
-            jax.ShapeDtypeStruct((2, PAIRS, rows, cols), jnp.float32),
-            jax.ShapeDtypeStruct((2, PAIRS, rows, cols), jnp.float32),
-            jax.ShapeDtypeStruct((2, PAIRS, rows, cols), jnp.float32),
+            jax.ShapeDtypeStruct((4, PAIRS, rows, cols), jnp.float32),
+            jax.ShapeDtypeStruct((4, PAIRS, rows, cols), jnp.float32),
+            jax.ShapeDtypeStruct((4, PAIRS, rows, cols), jnp.float32),
+            jax.ShapeDtypeStruct((4, PAIRS, rows, cols), jnp.float32),
             jax.ShapeDtypeStruct((rows, cols), jnp.float32),
         ),
         scratch_shapes=[
-            pltpu.VMEM((dim // 4, cols), jnp.float32),
+            pltpu.VMEM((dim, cols), jnp.float32),
             pltpu.VMEM(acts.shape, acts.dtype),
             pltpu.VMEM(cot.shape, cot.dtype),
             pltpu.VMEM(chosen.shape, chosen.dtype),
@@ -180,17 +189,21 @@
     away, near, kept_away, kept_near, mask = partials(
         activations[0], cotangent[0], components[0].transpose(1, 2, 0)
     )
-    core = partners(lambda core: (0, 0, 1))
-    once, twice = partners(lambda core: (core, 1 - core, 0)), partners(lambda core: (1 - core, core, 0))
+    core = partners("core", "core")
+    move_1, move_2, move_3 = partners("x", "across"), partners("across", "along"), partners("along", "x")
     away = lax.ppermute(away, "fsdp", core)
     near = add(kept_near, lax.ppermute(near, "fsdp", core))
-    two = lax.ppermute(kept_away[0] + away[0], "fsdp", once)
-    one = lax.ppermute(kept_away[1] + away[1], "fsdp", once)
-    here = add(near[1], one)
-    mine = here + lax.ppermute(near[0] + two, "fsdp", twice)
+    two = lax.ppermute(kept_away[:2] + away[:2], "fsdp", move_1)
+    one = lax.ppermute(kept_away[2:] + away[2:], "fsdp", move_1)
+    here = add(near[2:], one)
+    third = lax.ppermute(near[0] + two[0], "fsdp", move_2)
+    none = lax.ppermute(near[1] + two[1], "fsdp", move_2)
+    last = lax.ppermute(here[0] + third, "fsdp", move_3)
+    mine = add(here[1], none) + last
     members = [
-        [index_of(pair, group, x, core) for pair in range(PAIRS)]
-        for group in range(2)
+        [index_of(pair, side, kind, x, core) for pair in range(PAIRS)]
+        for side in range(2)
+        for kind in range(2)
         for x in range(2)
         for core in range(2)
     ]

time: 84.9 us -> 80.5 us (0.948)
  blocking collectives: 51 us -> 41.1 us
  starting transfers between devices: 17.7 us -> 21.4 us
  waiting for transfers between devices: 9.36 us -> 10.9 us
    all_to_all x1, blocking collectives: 34.6 us -> 24.8 us  [shards(): pieces = lax.all_to_all(mine, 'fsdp', 0, 0, axis_index_groups=members)]
    ppermute x3 -> x5, starting transfers between devices: 13.4 us -> 17.1 us  [the longest x1 7.39 us: shards(): third = lax.ppermute(near[0] + two[0], 'fsdp', move_2)]
    ppermute x3 -> x5, waiting for transfers between devices: 9.36 us -> 10.9 us  [the longest x1 3.69 us: shards(): two = lax.ppermute(kept_away[:2] + away[:2], 'fsdp', move_1)]
  transfers between devices with their start and end apart: 5 -> 7, of which waited for: 2 -> 4; matrix products, arithmetic and copies ran while one was open for 0% -> 0% of each run, Pallas kernels for 0% -> 0%
where the time goes in v5:
time: 80.5 us; the launch traced here: 80.1 us
  blocking collectives  41.1 us (51%)
  starting transfers between devices  21.4 us (27%)
  waiting for transfers between devices  10.9 us (14%)
  Pallas kernels  5.01 us (6%)
  other arithmetic  0.87 us (1%)
    all_to_all x1, blocking collectives, shards(): pieces = lax.all_to_all(mine, 'fsdp', 0, 0, axis_index_groups=members)  24.8 us
    all_to_all x1, blocking collectives, shards(): restored = lax.all_to_all(copies, 'rep', 0, 0)  16.3 us
    ppermute x1, starting transfers between devices, shards(): third = lax.ppermute(near[0] + two[0], 'fsdp', move_2)  7.39 us
    pallas_call x1, Pallas kernels, partials(): pl.pallas_call(partial_kernel, in_specs=[pl.BlockSpec(memory_space=pl.ANY...  3.85 us
    ppermute x1, waiting for transfers between devices, shards(): two = lax.ppermute(kept_away[:2] + away[:2], 'fsdp', move_1)  3.69 us
    ppermute x1, waiting for transfers between devices, shards(): last = lax.ppermute(here[0] + third, 'fsdp', move_3)  3.6 us
    ppermute x1, starting transfers between devices, shards(): two = lax.ppermute(kept_away[:2] + away[:2], 'fsdp', move_1)  3.4 us
    ppermute x1, starting transfers between devices, shards(): one = lax.ppermute(kept_away[2:] + away[2:], 'fsdp', move_1)  2.44 us
  transfers between devices with their start and end apart: 7, of which 4 were waited for; matrix products, arithmetic and copies ran while one was open for 0% of the time, Pallas kernels for 0%

profile of v5, /device:TPU:32, one launch (start us, length us, event | category | flops | bytes accessed | tf_op | source)
XLA Modules:
  0.0 80.1 jit_solution(16223818571130728983)
XLA Ops:
  0.6 3.9 %shard_map.68 = (f32[4,4,48,256]{3,2,1,0:T(8,128)S(1)}, f32[4,4,48,256]{3,2,1,0:T(8,128)S(1)}, f32[4,4,48,256]{3,2,1,0:T(8,128)S(1)}, f32[4,4,48,256]{3,2,1,0:T(8,128)S(1)}, f32[48,256]{1,0:T(8,128)S(1)}) custom-call(bf16[640,3072]{1,0:T(8,128)(2,1)} %bitcast.18, bf16[640,256]{1,0:T(8,128)(2,1)} %bitcast.19, s32[4,8,48]{2,1,0:T(8,128)} %bitcast.20), custom_call_target="tpu_custom_call" | custom-call | tf_op jit(solution)/shard_map/pallas_call | solution.py:110
  4.5 1.9 %collective-permute-start.1 = (f32[4,4,48,256]{3,2,1,0:T(8,128)S(1)}, f32[4,4,48,256]{3,2,1,0:T(8,128)S(1)}, u32[]{:S(2)}, u32[]{:S(2)}) collective-permute-start(f32[4,4,48,256]{3,2,1,0:T(8,128)S(1)} %get-tuple-element.12), channel_id=1, source_target_pairs={{0,1},{1,0},{2,3},{3,2},{4,5},{5,4},{6,7},{7,6},{8,9},{9,8},{10,11... | collective-permute-start | bytes 2359304 | tf_op jit(solution)/shard_map/ppermute | solution.py:194
  6.4 2.4 %collective-permute-start = (f32[4,4,48,256]{3,2,1,0:T(8,128)S(1)}, f32[4,4,48,256]{3,2,1,0:T(8,128)S(1)}, u32[]{:S(2)}, u32[]{:S(2)}) collective-permute-start(f32[4,4,48,256]{3,2,1,0:T(8,128)S(1)} %get-tuple-element.10), channel_id=1, source_target_pairs={{0,1},{1,0},{2,3},{3,2},{4,5},{5,4},{6,7},{7,6},{8,9},{9,8},{10,11... | collective-permute-start | bytes 2359304 | tf_op jit(solution)/shard_map/ppermute | solution.py:195
  8.8 0.0 collective-permute-done.1
  8.8 0.1 slice_add_fusion
  9.0 3.4 %collective-permute-start.3 = (f32[2,4,48,256]{3,2,1,0:T(8,128)S(1)}, f32[2,4,48,256]{3,2,1,0:T(8,128)S(1)}, u32[]{:S(2)}, u32[]{:S(2)}) collective-permute-start(f32[2,4,48,256]{3,2,1,0:T(8,128)S(1)} %get-tuple-element.16), channel_id=1, source_target_pairs={{0,2},{1,5},{2,0},{3,7},{4,6},{5,1},{6,4},{7,3},{8,10},{9,13},{10,... | collective-permute-start | bytes 1179656 | tf_op jit(solution)/shard_map/ppermute | solution.py:196
  12.4 2.4 %collective-permute-start.2 = (f32[2,4,48,256]{3,2,1,0:T(8,128)S(1)}, f32[2,4,48,256]{3,2,1,0:T(8,128)S(1)}, u32[]{:S(2)}, u32[]{:S(2)}) collective-permute-start(f32[2,4,48,256]{3,2,1,0:T(8,128)S(1)} %get-tuple-element.17), channel_id=1, source_target_pairs={{0,2},{1,5},{2,0},{3,7},{4,6},{5,1},{6,4},{7,3},{8,10},{9,13},{10,... | collective-permute-start | bytes 1179656 | tf_op jit(solution)/shard_map/ppermute | solution.py:197
  14.8 0.0 collective-permute-done.b_ref
  14.8 0.0 copy-start
  14.8 0.0 copy-start.1
  14.9 0.1 shard_map.69
  14.9 3.7 %collective-permute-done.3 = f32[2,4,48,256]{3,2,1,0:T(8,128)S(1)} collective-permute-done((f32[2,4,48,256]{3,2,1,0:T(8,128)S(1)}, f32[2,4,48,256]{3,2,1,0:T(8,128)S(1)}, u32[]{:S(2)}, u32[]{:S(2)}) %collective-permute-start.3) | collective-permute-done | bytes 393248 | tf_op jit(solution)/shard_map/ppermute | solution.py:196
  18.6 0.1 fusion
  18.7 7.4 %collective-permute-start.5 = (f32[4,48,256]{2,1,0:T(8,128)S(1)}, f32[4,48,256]{2,1,0:T(8,128)S(1)}, u32[]{:S(2)}, u32[]{:S(2)}) collective-permute-start(f32[4,48,256]{2,1,0:T(8,128)S(1)} %get-tuple-element.18), channel_id=1, source_target_pairs={{0,4},{1,61},{2,6},{3,63},{4,0},{5,9},{6,2},{7,11},{8,12},{9,5},{1... | collective-permute-start | bytes 589832 | tf_op jit(solution)/shard_map/ppermute | solution.py:199
  26.1 1.9 %collective-permute-start.4 = (f32[4,48,256]{2,1,0:T(8,128)S(1)}, f32[4,48,256]{2,1,0:T(8,128)S(1)}, u32[]{:S(2)}, u32[]{:S(2)}) collective-permute-start(f32[4,48,256]{2,1,0:T(8,128)S(1)} %get-tuple-element.19), channel_id=1, source_target_pairs={{0,4},{1,61},{2,6},{3,63},{4,0},{5,9},{6,2},{7,11},{8,12},{9,5},{1... | collective-permute-start | bytes 589832 | tf_op jit(solution)/shard_map/ppermute | solution.py:200
  28.0 0.0 collective-permute-done.2.b_ref
  28.1 1.6 %collective-permute-done.5 = f32[4,48,256]{2,1,0:T(8,128)S(1)} collective-permute-done((f32[4,48,256]{2,1,0:T(8,128)S(1)}, f32[4,48,256]{2,1,0:T(8,128)S(1)}, u32[]{:S(2)}, u32[]{:S(2)}) %collective-permute-start.5) | collective-permute-done | bytes 196640 | tf_op jit(solution)/shard_map/ppermute | solution.py:199
  29.7 1.9 %collective-permute-start.6 = (f32[4,48,256]{2,1,0:T(8,128)S(1)}, f32[4,48,256]{2,1,0:T(8,128)S(1)}, u32[]{:S(2)}, u32[]{:S(2)}) collective-permute-start(f32[4,48,256]{2,1,0:T(8,128)S(1)} %fusion.1), channel_id=1, source_target_pairs={{0,60},{1,3},{2,62},{3,1},{4,8},{5,7},{6,10},{7,5},{8,4},{9,11},{1... | collective-permute-start | bytes 589832 | tf_op jit(solution)/shard_map/ppermute | solution.py:201
  31.7 2.0 %collective-permute-done.4.b_ref = f32[4,48,256]{2,1,0:T(8,128)S(1)} collective-permute-done((f32[4,48,256]{2,1,0:T(8,128)S(1)}, f32[4,48,256]{2,1,0:T(8,128)S(1)}, u32[]{:S(2)}, u32[]{:S(2)}) %collective-permute-start.4) | collective-permute-done | bytes 196640 | tf_op jit(solution)/shard_map/ppermute | solution.py:200
  33.7 3.6 %collective-permute-done.6 = f32[4,48,256]{2,1,0:T(8,128)S(1)} collective-permute-done((f32[4,48,256]{2,1,0:T(8,128)S(1)}, f32[4,48,256]{2,1,0:T(8,128)S(1)}, u32[]{:S(2)}, u32[]{:S(2)}) %collective-permute-start.6) | collective-permute-done | bytes 196640 | tf_op jit(solution)/shard_map/ppermute | solution.py:201
  37.3 24.8 %all_to_all.10.pieces_ref = f32[4,48,256]{2,1,0:T(8,128)S(1)} all-to-all(f32[4,48,256]{2,1,0:T(8,128)S(1)} %add.31), channel_id=1, replica_groups={{12,28,48,0},{13,29,49,1},{14,30,50,2},{15,31,51,3},{4,20,40,56},{5,21,..., dimensions={0} | all-to-all | bytes 393216 | tf_op jit(solution)/shard_map/all_to_all | solution.py:210
  62.1 0.0 copy-done
  62.1 0.0 copy-done.1
  62.1 1.0 %shard_map.72 = (f32[48,256]{1,0:T(8,128)}, f32[8,48,256]{2,1,0:T(8,128)S(1)}) custom-call(f32[4,48,256]{2,1,0:T(8,128)S(1)} %all_to_all.10.pieces_ref, f32[48,256]{1,0:T(8,128)S(1)} %bitcast.17, f32[48,256]{1,0:T(8,128)S(1)} %get-tuple-element.13.mask_ref, bf16[2,256,256]{2,1,0:T(8,128)(2,1)S(1)} %copy-done), custom_call_target="tpu_custom_call" | custom-call | tf_op jit(solution)/shard_map/pallas_call | solution.py:164
  63.1 16.3 %all_to_all.11 = f32[8,48,256]{2,1,0:T(8,128)S(1)} all-to-all(f32[8,48,256]{2,1,0:T(8,128)S(1)} %get-tuple-element.14), channel_id=1, replica_groups=mesh['rep'=8,'fsdp'=64] {'rep'}, dimensions={0} | all-to-all | bytes 786432 | tf_op jit(solution)/shard_map/all_to_all | solution.py:212
  79.5 0.6 broadcast_multiply_fusion
  (7 shorter events, 0.2 us)
Async XLA Ops:
  4.5 4.3 %collective-permute-start.1 = (f32[4,4,48,256]{3,2,1,0:T(8,128)S(1)}, f32[4,4,48,256]{3,2,1,0:T(8,128)S(1)}, u32[]{:S(2)}, u32[]{:S(2)}) collective-permute-start(f32[4,4,48,256]{3,2,1,0:T(8,128)S(1)} %get-tuple-element.12), channel_id=1, source_target_pairs={{0,1},{1,0},{2,3},{3,2},{4,5},{5,4},{6,7},{7,6},{8,9},{9,8},{10,11... | collective-permute-start | bytes 2359304 | tf_op jit(solution)/shard_map/ppermute | solution.py:194
  6.4 8.4 %collective-permute-start = (f32[4,4,48,256]{3,2,1,0:T(8,128)S(1)}, f32[4,4,48,256]{3,2,1,0:T(8,128)S(1)}, u32[]{:S(2)}, u32[]{:S(2)}) collective-permute-start(f32[4,4,48,256]{3,2,1,0:T(8,128)S(1)} %get-tuple-element.10), channel_id=1, source_target_pairs={{0,1},{1,0},{2,3},{3,2},{4,5},{5,4},{6,7},{7,6},{8,9},{9,8},{10,11... | collective-permute-start | bytes 2359304 | tf_op jit(solution)/shard_map/ppermute | solution.py:195
  9.0 9.7 %collective-permute-start.3 = (f32[2,4,48,256]{3,2,1,0:T(8,128)S(1)}, f32[2,4,48,256]{3,2,1,0:T(8,128)S(1)}, u32[]{:S(2)}, u32[]{:S(2)}) collective-permute-start(f32[2,4,48,256]{3,2,1,0:T(8,128)S(1)} %get-tuple-element.16), channel_id=1, source_target_pairs={{0,2},{1,5},{2,0},{3,7},{4,6},{5,1},{6,4},{7,3},{8,10},{9,13},{10,... | collective-permute-start | bytes 1179656 | tf_op jit(solution)/shard_map/ppermute | solution.py:196
  12.4 15.7 %collective-permute-start.2 = (f32[2,4,48,256]{3,2,1,0:T(8,128)S(1)}, f32[2,4,48,256]{3,2,1,0:T(8,128)S(1)}, u32[]{:S(2)}, u32[]{:S(2)}) collective-permute-start(f32[2,4,48,256]{3,2,1,0:T(8,128)S(1)} %get-tuple-element.17), channel_id=1, source_target_pairs={{0,2},{1,5},{2,0},{3,7},{4,6},{5,1},{6,4},{7,3},{8,10},{9,13},{10,... | collective-permute-start | bytes 1179656 | tf_op jit(solution)/shard_map/ppermute | solution.py:197
  14.8 47.3 %copy-start = (bf16[2,256,256]{2,1,0:T(8,128)(2,1)S(1)}, bf16[2,256,256]{2,1,0:T(8,128)(2,1)}, u32[]{:S(2)}) copy-start(bf16[2,256,256]{2,1,0:T(8,128)(2,1)} %constant.7.clone.table_ref) | copy-start | bytes 786436
  14.8 47.3 %copy-start.1 = (f32[1,48,256]{2,1,0:T(8,128)S(1)}, f32[1,48,256]{2,1,0:T(8,128)}, u32[]{:S(2)}) copy-start(f32[1,48,256]{2,1,0:T(8,128)} %param.7) | copy-start | bytes 147460
  18.7 11.0 %collective-permute-start.5 = (f32[4,48,256]{2,1,0:T(8,128)S(1)}, f32[4,48,256]{2,1,0:T(8,128)S(1)}, u32[]{:S(2)}, u32[]{:S(2)}) collective-permute-start(f32[4,48,256]{2,1,0:T(8,128)S(1)} %get-tuple-element.18), channel_id=1, source_target_pairs={{0,4},{1,61},{2,6},{3,63},{4,0},{5,9},{6,2},{7,11},{8,12},{9,5},{1... | collective-permute-start | bytes 589832 | tf_op jit(solution)/shard_map/ppermute | solution.py:199
  26.1 7.6 %collective-permute-start.4 = (f32[4,48,256]{2,1,0:T(8,128)S(1)}, f32[4,48,256]{2,1,0:T(8,128)S(1)}, u32[]{:S(2)}, u32[]{:S(2)}) collective-permute-start(f32[4,48,256]{2,1,0:T(8,128)S(1)} %get-tuple-element.19), channel_id=1, source_target_pairs={{0,4},{1,61},{2,6},{3,63},{4,0},{5,9},{6,2},{7,11},{8,12},{9,5},{1... | collective-permute-start | bytes 589832 | tf_op jit(solution)/shard_map/ppermute | solution.py:200
  29.7 7.6 %collective-permute-start.6 = (f32[4,48,256]{2,1,0:T(8,128)S(1)}, f32[4,48,256]{2,1,0:T(8,128)S(1)}, u32[]{:S(2)}, u32[]{:S(2)}) collective-permute-start(f32[4,48,256]{2,1,0:T(8,128)S(1)} %fusion.1), channel_id=1, source_target_pairs={{0,60},{1,3},{2,62},{3,1},{4,8},{5,7},{6,10},{7,5},{8,4},{9,11},{1... | collective-permute-start | bytes 589832 | tf_op jit(solution)/shard_map/ppermute | solution.py:201

commit v6 on v5

--- a/solution.py
+++ b/solution.py
@@ -193,13 +193,14 @@
     move_1, move_2, move_3 = partners("x", "across"), partners("across", "along"), partners("along", "x")
     away = lax.ppermute(away, "fsdp", core)
     near = add(kept_near, lax.ppermute(near, "fsdp", core))
-    two = lax.ppermute(kept_away[:2] + away[:2], "fsdp", move_1)
-    one = lax.ppermute(kept_away[2:] + away[2:], "fsdp", move_1)
-    here = add(near[2:], one)
-    third = lax.ppermute(near[0] + two[0], "fsdp", move_2)
-    none = lax.ppermute(near[1] + two[1], "fsdp", move_2)
-    last = lax.ppermute(here[0] + third, "fsdp", move_3)
-    mine = add(here[1], none) + last
+    both = lax.ppermute(kept_away[0] + away[0], "fsdp", move_1)
+    either = lax.ppermute(kept_away[1:3] + away[1:3], "fsdp", move_1)
+    none = lax.ppermute(kept_away[3] + away[3], "fsdp", move_1)
+    third = lax.ppermute(near[0] + both, "fsdp", move_2)
+    here = add(near[2], either[1])
+    ready = lax.ppermute(near[1] + either[0], "fsdp", move_2)
+    last = lax.ppermute(here + third, "fsdp", move_3)
+    mine = add(add(near[3], none), ready) + last
     members = [
         [index_of(pair, side, kind, x, core) for pair in range(PAIRS)]
         for side in range(2)

time: 80.5 us -> 79.9 us (level)
  waiting for transfers between devices: 10.9 us -> 6.39 us
  starting transfers between devices: 21.4 us -> 25.1 us
    ppermute x5 -> x6, waiting for transfers between devices: 10.9 us -> 6.39 us  [the longest x1 4.57 us: shards(): last = lax.ppermute(here + third, 'fsdp', move_3)]
    ppermute x5 -> x6, starting transfers between devices: 17.1 us -> 20.8 us  [the longest x1 5.91 us: shards(): third = lax.ppermute(near[0] + both, 'fsdp', move_2)]
  transfers between devices with their start and end apart: 7 -> 8, of which waited for: 4 -> 3; matrix products, arithmetic and copies ran while one was open for 0% -> 0% of each run, Pallas kernels for 0% -> 0%
where the time goes in v6:
time: 79.9 us; the launch traced here: 79.5 us
  blocking collectives  41.2 us (52%)
  starting transfers between devices  25.1 us (31%)
  waiting for transfers between devices  6.39 us (8%)
  Pallas kernels  5.04 us (6%)
  other arithmetic  0.93 us (1%)
  between operations  0.81 us (1%)
    all_to_all x1, blocking collectives, shards(): pieces = lax.all_to_all(mine, 'fsdp', 0, 0, axis_index_groups=members)  25 us
    all_to_all x1, blocking collectives, shards(): restored = lax.all_to_all(copies, 'rep', 0, 0)  16.2 us
    ppermute x1, starting transfers between devices, shards(): third = lax.ppermute(near[0] + both, 'fsdp', move_2)  5.91 us
    ppermute x1, waiting for transfers between devices, shards(): last = lax.ppermute(here + third, 'fsdp', move_3)  4.57 us
    pallas_call x1, Pallas kernels, partials(): pl.pallas_call(partial_kernel, in_specs=[pl.BlockSpec(memory_space=pl.ANY...  3.85 us
    ppermute x1, starting transfers between devices, shards(): ready = lax.ppermute(near[1] + either[0], 'fsdp', move_2)  3.71 us
    ppermute x1, starting transfers between devices, shards(): both = lax.ppermute(kept_away[0] + away[0], 'fsdp', move_1)  3.4 us
    ppermute x1, starting transfers between devices, shards(): none = lax.ppermute(kept_away[3] + away[3], 'fsdp', move_1)  3.4 us
  transfers between devices with their start and end apart: 8, of which 3 were waited for; matrix products, arithmetic and copies ran while one was open for 0% of the time, Pallas kernels for 0%

profile of v6, /device:TPU:32, one launch (start us, length us, event | category | flops | bytes accessed | tf_op | source)
XLA Modules:
  0.0 79.5 jit_solution(6500830719600754864)
XLA Ops:
  0.6 3.9 %shard_map.68 = (f32[4,4,48,256]{3,2,1,0:T(8,128)S(1)}, f32[4,4,48,256]{3,2,1,0:T(8,128)S(1)}, f32[4,4,48,256]{3,2,1,0:T(8,128)S(1)}, f32[4,4,48,256]{3,2,1,0:T(8,128)S(1)}, f32[48,256]{1,0:T(8,128)S(1)}) custom-call(bf16[640,3072]{1,0:T(8,128)(2,1)} %bitcast.24, bf16[640,256]{1,0:T(8,128)(2,1)} %bitcast.25, s32[4,8,48]{2,1,0:T(8,128)} %bitcast.26), custom_call_target="tpu_custom_call" | custom-call | tf_op jit(solution)/shard_map/pallas_call | solution.py:110
  4.5 1.9 %collective-permute-start.1 = (f32[4,4,48,256]{3,2,1,0:T(8,128)S(1)}, f32[4,4,48,256]{3,2,1,0:T(8,128)S(1)}, u32[]{:S(2)}, u32[]{:S(2)}) collective-permute-start(f32[4,4,48,256]{3,2,1,0:T(8,128)S(1)} %get-tuple-element.12), channel_id=1, source_target_pairs={{0,1},{1,0},{2,3},{3,2},{4,5},{5,4},{6,7},{7,6},{8,9},{9,8},{10,11... | collective-permute-start | bytes 2359304 | tf_op jit(solution)/shard_map/ppermute | solution.py:194
  6.4 2.4 %collective-permute-start = (f32[4,4,48,256]{3,2,1,0:T(8,128)S(1)}, f32[4,4,48,256]{3,2,1,0:T(8,128)S(1)}, u32[]{:S(2)}, u32[]{:S(2)}) collective-permute-start(f32[4,4,48,256]{3,2,1,0:T(8,128)S(1)} %get-tuple-element.10), channel_id=1, source_target_pairs={{0,1},{1,0},{2,3},{3,2},{4,5},{5,4},{6,7},{7,6},{8,9},{9,8},{10,11... | collective-permute-start | bytes 2359304 | tf_op jit(solution)/shard_map/ppermute | solution.py:195
  8.8 0.0 collective-permute-done.1
  8.8 0.1 fusion
  8.9 3.4 %collective-permute-start.5 = (f32[4,48,256]{2,1,0:T(8,128)S(1)}, f32[4,48,256]{2,1,0:T(8,128)S(1)}, u32[]{:S(2)}, u32[]{:S(2)}) collective-permute-start(f32[4,48,256]{2,1,0:T(8,128)S(1)} %get-tuple-element.16), channel_id=1, source_target_pairs={{0,2},{1,5},{2,0},{3,7},{4,6},{5,1},{6,4},{7,3},{8,10},{9,13},{10,... | collective-permute-start | bytes 589832 | tf_op jit(solution)/shard_map/ppermute | solution.py:196
  12.3 0.1 slice_add_fusion
  12.4 2.4 %collective-permute-start.3 = (f32[2,4,48,256]{3,2,1,0:T(8,128)S(1)}, f32[2,4,48,256]{3,2,1,0:T(8,128)S(1)}, u32[]{:S(2)}, u32[]{:S(2)}) collective-permute-start(f32[2,4,48,256]{3,2,1,0:T(8,128)S(1)} %slice_add_fusion), channel_id=1, source_target_pairs={{0,2},{1,5},{2,0},{3,7},{4,6},{5,1},{6,4},{7,3},{8,10},{9,13},{10,... | collective-permute-start | bytes 1179656 | tf_op jit(solution)/shard_map/ppermute | solution.py:197
  14.8 3.4 %collective-permute-start.2 = (f32[4,48,256]{2,1,0:T(8,128)S(1)}, f32[4,48,256]{2,1,0:T(8,128)S(1)}, u32[]{:S(2)}, u32[]{:S(2)}) collective-permute-start(f32[4,48,256]{2,1,0:T(8,128)S(1)} %get-tuple-element.17), channel_id=1, source_target_pairs={{0,2},{1,5},{2,0},{3,7},{4,6},{5,1},{6,4},{7,3},{8,10},{9,13},{10,... | collective-permute-start | bytes 589832 | tf_op jit(solution)/shard_map/ppermute | solution.py:198
  18.2 0.0 collective-permute-done.b_ref
  18.2 0.0 copy-start
  18.3 0.0 copy-start.1
  18.3 0.1 shard_map.69
  18.4 0.0 collective-permute-done.5
  18.4 5.9 %collective-permute-start.6 = (f32[4,48,256]{2,1,0:T(8,128)S(1)}, f32[4,48,256]{2,1,0:T(8,128)S(1)}, u32[]{:S(2)}, u32[]{:S(2)}) collective-permute-start(f32[4,48,256]{2,1,0:T(8,128)S(1)} %fusion.1), channel_id=1, source_target_pairs={{0,4},{1,61},{2,6},{3,63},{4,0},{5,9},{6,2},{7,11},{8,12},{9,5},{1... | collective-permute-start | bytes 589832 | tf_op jit(solution)/shard_map/ppermute | solution.py:199
  24.3 0.0 collective-permute-done.3
  24.4 0.1 slice_bitcast_fusion.2
  24.4 3.7 %collective-permute-start.4 = (f32[4,48,256]{2,1,0:T(8,128)S(1)}, f32[4,48,256]{2,1,0:T(8,128)S(1)}, u32[]{:S(2)}, u32[]{:S(2)}) collective-permute-start(f32[4,48,256]{2,1,0:T(8,128)S(1)} %get-tuple-element.19), channel_id=1, source_target_pairs={{0,4},{1,61},{2,6},{3,63},{4,0},{5,9},{6,2},{7,11},{8,12},{9,5},{1... | collective-permute-start | bytes 589832 | tf_op jit(solution)/shard_map/ppermute | solution.py:201
  28.2 0.8 %collective-permute-done.6 = f32[4,48,256]{2,1,0:T(8,128)S(1)} collective-permute-done((f32[4,48,256]{2,1,0:T(8,128)S(1)}, f32[4,48,256]{2,1,0:T(8,128)S(1)}, u32[]{:S(2)}, u32[]{:S(2)}) %collective-permute-start.6) | collective-permute-done | bytes 196640 | tf_op jit(solution)/shard_map/ppermute | solution.py:199
  29.0 1.9 %collective-permute-start.7 = (f32[4,48,256]{2,1,0:T(8,128)S(1)}, f32[4,48,256]{2,1,0:T(8,128)S(1)}, u32[]{:S(2)}, u32[]{:S(2)}) collective-permute-start(f32[4,48,256]{2,1,0:T(8,128)S(1)} %add.38), channel_id=1, source_target_pairs={{0,60},{1,3},{2,62},{3,1},{4,8},{5,7},{6,10},{7,5},{8,4},{9,11},{1... | collective-permute-start | bytes 589832 | tf_op jit(solution)/shard_map/ppermute | solution.py:202
  31.0 0.0 collective-permute-done.2.b_ref
  31.0 1.0 %collective-permute-done.4.b_ref = f32[4,48,256]{2,1,0:T(8,128)S(1)} collective-permute-done((f32[4,48,256]{2,1,0:T(8,128)S(1)}, f32[4,48,256]{2,1,0:T(8,128)S(1)}, u32[]{:S(2)}, u32[]{:S(2)}) %collective-permute-start.4) | collective-permute-done | bytes 196640 | tf_op jit(solution)/shard_map/ppermute | solution.py:201
  32.0 4.6 %collective-permute-done.7 = f32[4,48,256]{2,1,0:T(8,128)S(1)} collective-permute-done((f32[4,48,256]{2,1,0:T(8,128)S(1)}, f32[4,48,256]{2,1,0:T(8,128)S(1)}, u32[]{:S(2)}, u32[]{:S(2)}) %collective-permute-start.7) | collective-permute-done | bytes 196640 | tf_op jit(solution)/shard_map/ppermute | solution.py:202
  36.6 25.0 %all_to_all.10.pieces_ref = f32[4,48,256]{2,1,0:T(8,128)S(1)} all-to-all(f32[4,48,256]{2,1,0:T(8,128)S(1)} %add.39), channel_id=1, replica_groups={{12,28,48,0},{13,29,49,1},{14,30,50,2},{15,31,51,3},{4,20,40,56},{5,21,..., dimensions={0} | all-to-all | bytes 393216 | tf_op jit(solution)/shard_map/all_to_all | solution.py:211
  61.6 0.0 copy-done
  61.6 0.0 copy-done.1
  61.6 1.0 %shard_map.73 = (f32[48,256]{1,0:T(8,128)}, f32[8,48,256]{2,1,0:T(8,128)S(1)}) custom-call(f32[4,48,256]{2,1,0:T(8,128)S(1)} %all_to_all.10.pieces_ref, f32[48,256]{1,0:T(8,128)S(1)} %bitcast.23, f32[48,256]{1,0:T(8,128)S(1)} %get-tuple-element.13.mask_ref, bf16[2,256,256]{2,1,0:T(8,128)(2,1)S(1)} %copy-done), custom_call_target="tpu_custom_call" | custom-call | tf_op jit(solution)/shard_map/pallas_call | solution.py:164
  62.6 16.2 %all_to_all.11 = f32[8,48,256]{2,1,0:T(8,128)S(1)} all-to-all(f32[8,48,256]{2,1,0:T(8,128)S(1)} %get-tuple-element.14), channel_id=1, replica_groups=mesh['rep'=8,'fsdp'=64] {'rep'}, dimensions={0} | all-to-all | bytes 786432 | tf_op jit(solution)/shard_map/all_to_all | solution.py:213
  78.9 0.6 broadcast_multiply_fusion
  (7 shorter events, 0.2 us)
Async XLA Ops:
  4.5 4.3 %collective-permute-start.1 = (f32[4,4,48,256]{3,2,1,0:T(8,128)S(1)}, f32[4,4,48,256]{3,2,1,0:T(8,128)S(1)}, u32[]{:S(2)}, u32[]{:S(2)}) collective-permute-start(f32[4,4,48,256]{3,2,1,0:T(8,128)S(1)} %get-tuple-element.12), channel_id=1, source_target_pairs={{0,1},{1,0},{2,3},{3,2},{4,5},{5,4},{6,7},{7,6},{8,9},{9,8},{10,11... | collective-permute-start | bytes 2359304 | tf_op jit(solution)/shard_map/ppermute | solution.py:194
  6.4 11.8 %collective-permute-start = (f32[4,4,48,256]{3,2,1,0:T(8,128)S(1)}, f32[4,4,48,256]{3,2,1,0:T(8,128)S(1)}, u32[]{:S(2)}, u32[]{:S(2)}) collective-permute-start(f32[4,4,48,256]{3,2,1,0:T(8,128)S(1)} %get-tuple-element.10), channel_id=1, source_target_pairs={{0,1},{1,0},{2,3},{3,2},{4,5},{5,4},{6,7},{7,6},{8,9},{9,8},{10,11... | collective-permute-start | bytes 2359304 | tf_op jit(solution)/shard_map/ppermute | solution.py:195
  8.9 9.5 %collective-permute-start.5 = (f32[4,48,256]{2,1,0:T(8,128)S(1)}, f32[4,48,256]{2,1,0:T(8,128)S(1)}, u32[]{:S(2)}, u32[]{:S(2)}) collective-permute-start(f32[4,48,256]{2,1,0:T(8,128)S(1)} %get-tuple-element.16), channel_id=1, source_target_pairs={{0,2},{1,5},{2,0},{3,7},{4,6},{5,1},{6,4},{7,3},{8,10},{9,13},{10,... | collective-permute-start | bytes 589832 | tf_op jit(solution)/shard_map/ppermute | solution.py:196
  12.4 12.0 %collective-permute-start.3 = (f32[2,4,48,256]{3,2,1,0:T(8,128)S(1)}, f32[2,4,48,256]{3,2,1,0:T(8,128)S(1)}, u32[]{:S(2)}, u32[]{:S(2)}) collective-permute-start(f32[2,4,48,256]{3,2,1,0:T(8,128)S(1)} %slice_add_fusion), channel_id=1, source_target_pairs={{0,2},{1,5},{2,0},{3,7},{4,6},{5,1},{6,4},{7,3},{8,10},{9,13},{10,... | collective-permute-start | bytes 1179656 | tf_op jit(solution)/shard_map/ppermute | solution.py:197
  14.8 16.1 %collective-permute-start.2 = (f32[4,48,256]{2,1,0:T(8,128)S(1)}, f32[4,48,256]{2,1,0:T(8,128)S(1)}, u32[]{:S(2)}, u32[]{:S(2)}) collective-permute-start(f32[4,48,256]{2,1,0:T(8,128)S(1)} %get-tuple-element.17), channel_id=1, source_target_pairs={{0,2},{1,5},{2,0},{3,7},{4,6},{5,1},{6,4},{7,3},{8,10},{9,13},{10,... | collective-permute-start | bytes 589832 | tf_op jit(solution)/shard_map/ppermute | solution.py:198
  18.2 43.4 %copy-start = (bf16[2,256,256]{2,1,0:T(8,128)(2,1)S(1)}, bf16[2,256,256]{2,1,0:T(8,128)(2,1)}, u32[]{:S(2)}) copy-start(bf16[2,256,256]{2,1,0:T(8,128)(2,1)} %constant.7.clone.table_ref) | copy-start | bytes 786436
  18.3 43.4 %copy-start.1 = (f32[1,48,256]{2,1,0:T(8,128)S(1)}, f32[1,48,256]{2,1,0:T(8,128)}, u32[]{:S(2)}) copy-start(f32[1,48,256]{2,1,0:T(8,128)} %param.7) | copy-start | bytes 147460
  18.4 10.6 %collective-permute-start.6 = (f32[4,48,256]{2,1,0:T(8,128)S(1)}, f32[4,48,256]{2,1,0:T(8,128)S(1)}, u32[]{:S(2)}, u32[]{:S(2)}) collective-permute-start(f32[4,48,256]{2,1,0:T(8,128)S(1)} %fusion.1), channel_id=1, source_target_pairs={{0,4},{1,61},{2,6},{3,63},{4,0},{5,9},{6,2},{7,11},{8,12},{9,5},{1... | collective-permute-start | bytes 589832 | tf_op jit(solution)/shard_map/ppermute | solution.py:199
  24.4 7.6 %collective-permute-start.4 = (f32[4,48,256]{2,1,0:T(8,128)S(1)}, f32[4,48,256]{2,1,0:T(8,128)S(1)}, u32[]{:S(2)}, u32[]{:S(2)}) collective-permute-start(f32[4,48,256]{2,1,0:T(8,128)S(1)} %get-tuple-element.19), channel_id=1, source_target_pairs={{0,4},{1,61},{2,6},{3,63},{4,0},{5,9},{6,2},{7,11},{8,12},{9,5},{1... | collective-permute-start | bytes 589832 | tf_op jit(solution)/shard_map/ppermute | solution.py:201
  29.0 7.6 %collective-permute-start.7 = (f32[4,48,256]{2,1,0:T(8,128)S(1)}, f32[4,48,256]{2,1,0:T(8,128)S(1)}, u32[]{:S(2)}, u32[]{:S(2)}) collective-permute-start(f32[4,48,256]{2,1,0:T(8,128)S(1)} %add.38), channel_id=1, source_target_pairs={{0,60},{1,3},{2,62},{3,1},{4,8},{5,7},{6,10},{7,5},{8,4},{9,11},{1... | collective-permute-start | bytes 589832 | tf_op jit(solution)/shard_map/ppermute | solution.py:202

commit v7 on v6

--- a/solution.py
+++ b/solution.py
@@ -63,10 +63,10 @@
     copy_chosen.start()
     copy_cot = pltpu.make_async_copy(cot_hbm, cot, cot_sem)
     copy_cot.start()
-    half = acts.shape[1] // 2
+    quarter, whole = acts.shape[1] // 4, acts.shape[1]
     copies = [
-        pltpu.make_async_copy(acts_hbm.at[:, pl.ds(at, half)], acts.at[:, pl.ds(at, half)], acts_sem.at[at // half])
-        for at in (0, half)
+        pltpu.make_async_copy(acts_hbm.at[:, pl.ds(at, size)], acts.at[:, pl.ds(at, size)], acts_sem.at[number])
+        for number, (at, size) in enumerate(((0, quarter), (quarter, whole - quarter)))
     ]
     for copy in copies:
         copy.start()
@@ -87,8 +87,8 @@
     turned = cot[...].T
     width = acts.shape[1] // 4
     for step in range(4):
-        if step % 2 == 0:
-            copies[step // 2].wait()
+        if step < 2:
+            copies[step].wait()
         product[step * width : (step + 1) * width] = jnp.dot(
             turned, acts[:, step * width : (step + 1) * width], preferred_element_type=jnp.float32
         ).T

time: 79.9 us -> 79.8 us (level)
  no operation moved by 1% of the time
where the time goes in v7:
time: 79.8 us; the launch traced here: 79.4 us
  blocking collectives  41.2 us (52%)
  starting transfers between devices  25.1 us (31%)
  waiting for transfers between devices  6.39 us (8%)
  Pallas kernels  4.94 us (6%)
  other arithmetic  0.93 us (1%)
  between operations  0.81 us (1%)
    all_to_all x1, blocking collectives, shards(): pieces = lax.all_to_all(mine, 'fsdp', 0, 0, axis_index_groups=members)  25 us
    all_to_all x1, blocking collectives, shards(): restored = lax.all_to_all(copies, 'rep', 0, 0)  16.2 us
    ppermute x1, starting transfers between devices, shards(): third = lax.ppermute(near[0] + both, 'fsdp', move_2)  5.91 us
    ppermute x1, waiting for transfers between devices, shards(): last = lax.ppermute(here + third, 'fsdp', move_3)  4.57 us
    pallas_call x1, Pallas kernels, partials(): pl.pallas_call(partial_kernel, in_specs=[pl.BlockSpec(memory_space=pl.ANY...  3.75 us
    ppermute x1, starting transfers between devices, shards(): ready = lax.ppermute(near[1] + either[0], 'fsdp', move_2)  3.71 us
    ppermute x1, starting transfers between devices, shards(): both = lax.ppermute(kept_away[0] + away[0], 'fsdp', move_1)  3.4 us
    ppermute x1, starting transfers between devices, shards(): none = lax.ppermute(kept_away[3] + away[3], 'fsdp', move_1)  3.4 us
  transfers between devices with their start and end apart: 8, of which 3 were waited for; matrix products, arithmetic and copies ran while one was open for 0% of the time, Pallas kernels for 0%

profile of v7, /device:TPU:32, one launch (start us, length us, event | category | flops | bytes accessed | tf_op | source)
XLA Modules:
  0.0 79.4 jit_solution(13213951380563145151)
XLA Ops:
  0.6 3.8 %shard_map.68 = (f32[4,4,48,256]{3,2,1,0:T(8,128)S(1)}, f32[4,4,48,256]{3,2,1,0:T(8,128)S(1)}, f32[4,4,48,256]{3,2,1,0:T(8,128)S(1)}, f32[4,4,48,256]{3,2,1,0:T(8,128)S(1)}, f32[48,256]{1,0:T(8,128)S(1)}) custom-call(bf16[640,3072]{1,0:T(8,128)(2,1)} %bitcast.24, bf16[640,256]{1,0:T(8,128)(2,1)} %bitcast.25, s32[4,8,48]{2,1,0:T(8,128)} %bitcast.26), custom_call_target="tpu_custom_call" | custom-call | tf_op jit(solution)/shard_map/pallas_call | solution.py:110
  4.4 1.9 %collective-permute-start.1 = (f32[4,4,48,256]{3,2,1,0:T(8,128)S(1)}, f32[4,4,48,256]{3,2,1,0:T(8,128)S(1)}, u32[]{:S(2)}, u32[]{:S(2)}) collective-permute-start(f32[4,4,48,256]{3,2,1,0:T(8,128)S(1)} %get-tuple-element.12), channel_id=1, source_target_pairs={{0,1},{1,0},{2,3},{3,2},{4,5},{5,4},{6,7},{7,6},{8,9},{9,8},{10,11... | collective-permute-start | bytes 2359304 | tf_op jit(solution)/shard_map/ppermute | solution.py:194
  6.3 2.4 %collective-permute-start = (f32[4,4,48,256]{3,2,1,0:T(8,128)S(1)}, f32[4,4,48,256]{3,2,1,0:T(8,128)S(1)}, u32[]{:S(2)}, u32[]{:S(2)}) collective-permute-start(f32[4,4,48,256]{3,2,1,0:T(8,128)S(1)} %get-tuple-element.10), channel_id=1, source_target_pairs={{0,1},{1,0},{2,3},{3,2},{4,5},{5,4},{6,7},{7,6},{8,9},{9,8},{10,11... | collective-permute-start | bytes 2359304 | tf_op jit(solution)/shard_map/ppermute | solution.py:195
  8.7 0.0 collective-permute-done.1
  8.7 0.1 fusion
  8.8 3.4 %collective-permute-start.5 = (f32[4,48,256]{2,1,0:T(8,128)S(1)}, f32[4,48,256]{2,1,0:T(8,128)S(1)}, u32[]{:S(2)}, u32[]{:S(2)}) collective-permute-start(f32[4,48,256]{2,1,0:T(8,128)S(1)} %get-tuple-element.16), channel_id=1, source_target_pairs={{0,2},{1,5},{2,0},{3,7},{4,6},{5,1},{6,4},{7,3},{8,10},{9,13},{10,... | collective-permute-start | bytes 589832 | tf_op jit(solution)/shard_map/ppermute | solution.py:196
  12.2 0.1 slice_add_fusion
  12.3 2.4 %collective-permute-start.3 = (f32[2,4,48,256]{3,2,1,0:T(8,128)S(1)}, f32[2,4,48,256]{3,2,1,0:T(8,128)S(1)}, u32[]{:S(2)}, u32[]{:S(2)}) collective-permute-start(f32[2,4,48,256]{3,2,1,0:T(8,128)S(1)} %slice_add_fusion), channel_id=1, source_target_pairs={{0,2},{1,5},{2,0},{3,7},{4,6},{5,1},{6,4},{7,3},{8,10},{9,13},{10,... | collective-permute-start | bytes 1179656 | tf_op jit(solution)/shard_map/ppermute | solution.py:197
  14.7 3.4 %collective-permute-start.2 = (f32[4,48,256]{2,1,0:T(8,128)S(1)}, f32[4,48,256]{2,1,0:T(8,128)S(1)}, u32[]{:S(2)}, u32[]{:S(2)}) collective-permute-start(f32[4,48,256]{2,1,0:T(8,128)S(1)} %get-tuple-element.17), channel_id=1, source_target_pairs={{0,2},{1,5},{2,0},{3,7},{4,6},{5,1},{6,4},{7,3},{8,10},{9,13},{10,... | collective-permute-start | bytes 589832 | tf_op jit(solution)/shard_map/ppermute | solution.py:198
  18.1 0.0 collective-permute-done.b_ref
  18.1 0.0 copy-start
  18.2 0.0 copy-start.1
  18.2 0.1 shard_map.69
  18.3 0.0 collective-permute-done.5
  18.3 5.9 %collective-permute-start.6 = (f32[4,48,256]{2,1,0:T(8,128)S(1)}, f32[4,48,256]{2,1,0:T(8,128)S(1)}, u32[]{:S(2)}, u32[]{:S(2)}) collective-permute-start(f32[4,48,256]{2,1,0:T(8,128)S(1)} %fusion.1), channel_id=1, source_target_pairs={{0,4},{1,61},{2,6},{3,63},{4,0},{5,9},{6,2},{7,11},{8,12},{9,5},{1... | collective-permute-start | bytes 589832 | tf_op jit(solution)/shard_map/ppermute | solution.py:199
  24.2 0.0 collective-permute-done.3
  24.3 0.1 slice_bitcast_fusion.2
  24.3 3.7 %collective-permute-start.4 = (f32[4,48,256]{2,1,0:T(8,128)S(1)}, f32[4,48,256]{2,1,0:T(8,128)S(1)}, u32[]{:S(2)}, u32[]{:S(2)}) collective-permute-start(f32[4,48,256]{2,1,0:T(8,128)S(1)} %get-tuple-element.19), channel_id=1, source_target_pairs={{0,4},{1,61},{2,6},{3,63},{4,0},{5,9},{6,2},{7,11},{8,12},{9,5},{1... | collective-permute-start | bytes 589832 | tf_op jit(solution)/shard_map/ppermute | solution.py:201
  28.1 0.8 %collective-permute-done.6 = f32[4,48,256]{2,1,0:T(8,128)S(1)} collective-permute-done((f32[4,48,256]{2,1,0:T(8,128)S(1)}, f32[4,48,256]{2,1,0:T(8,128)S(1)}, u32[]{:S(2)}, u32[]{:S(2)}) %collective-permute-start.6) | collective-permute-done | bytes 196640 | tf_op jit(solution)/shard_map/ppermute | solution.py:199
  28.9 1.9 %collective-permute-start.7 = (f32[4,48,256]{2,1,0:T(8,128)S(1)}, f32[4,48,256]{2,1,0:T(8,128)S(1)}, u32[]{:S(2)}, u32[]{:S(2)}) collective-permute-start(f32[4,48,256]{2,1,0:T(8,128)S(1)} %add.38), channel_id=1, source_target_pairs={{0,60},{1,3},{2,62},{3,1},{4,8},{5,7},{6,10},{7,5},{8,4},{9,11},{1... | collective-permute-start | bytes 589832 | tf_op jit(solution)/shard_map/ppermute | solution.py:202
  30.9 0.0 collective-permute-done.2.b_ref
  30.9 1.0 %collective-permute-done.4.b_ref = f32[4,48,256]{2,1,0:T(8,128)S(1)} collective-permute-done((f32[4,48,256]{2,1,0:T(8,128)S(1)}, f32[4,48,256]{2,1,0:T(8,128)S(1)}, u32[]{:S(2)}, u32[]{:S(2)}) %collective-permute-start.4) | collective-permute-done | bytes 196640 | tf_op jit(solution)/shard_map/ppermute | solution.py:201
  31.9 4.6 %collective-permute-done.7 = f32[4,48,256]{2,1,0:T(8,128)S(1)} collective-permute-done((f32[4,48,256]{2,1,0:T(8,128)S(1)}, f32[4,48,256]{2,1,0:T(8,128)S(1)}, u32[]{:S(2)}, u32[]{:S(2)}) %collective-permute-start.7) | collective-permute-done | bytes 196640 | tf_op jit(solution)/shard_map/ppermute | solution.py:202
  36.5 25.0 %all_to_all.10.pieces_ref = f32[4,48,256]{2,1,0:T(8,128)S(1)} all-to-all(f32[4,48,256]{2,1,0:T(8,128)S(1)} %add.39), channel_id=1, replica_groups={{12,28,48,0},{13,29,49,1},{14,30,50,2},{15,31,51,3},{4,20,40,56},{5,21,..., dimensions={0} | all-to-all | bytes 393216 | tf_op jit(solution)/shard_map/all_to_all | solution.py:211
  61.5 0.0 copy-done
  61.5 0.0 copy-done.1
  61.5 1.0 %shard_map.73 = (f32[48,256]{1,0:T(8,128)}, f32[8,48,256]{2,1,0:T(8,128)S(1)}) custom-call(f32[4,48,256]{2,1,0:T(8,128)S(1)} %all_to_all.10.pieces_ref, f32[48,256]{1,0:T(8,128)S(1)} %bitcast.23, f32[48,256]{1,0:T(8,128)S(1)} %get-tuple-element.13.mask_ref, bf16[2,256,256]{2,1,0:T(8,128)(2,1)S(1)} %copy-done), custom_call_target="tpu_custom_call" | custom-call | tf_op jit(solution)/shard_map/pallas_call | solution.py:164
  62.5 16.2 %all_to_all.11 = f32[8,48,256]{2,1,0:T(8,128)S(1)} all-to-all(f32[8,48,256]{2,1,0:T(8,128)S(1)} %get-tuple-element.14), channel_id=1, replica_groups=mesh['rep'=8,'fsdp'=64] {'rep'}, dimensions={0} | all-to-all | bytes 786432 | tf_op jit(solution)/shard_map/all_to_all | solution.py:213
  78.8 0.6 broadcast_multiply_fusion
  (7 shorter events, 0.2 us)
Async XLA Ops:
  4.4 4.3 %collective-permute-start.1 = (f32[4,4,48,256]{3,2,1,0:T(8,128)S(1)}, f32[4,4,48,256]{3,2,1,0:T(8,128)S(1)}, u32[]{:S(2)}, u32[]{:S(2)}) collective-permute-start(f32[4,4,48,256]{3,2,1,0:T(8,128)S(1)} %get-tuple-element.12), channel_id=1, source_target_pairs={{0,1},{1,0},{2,3},{3,2},{4,5},{5,4},{6,7},{7,6},{8,9},{9,8},{10,11... | collective-permute-start | bytes 2359304 | tf_op jit(solution)/shard_map/ppermute | solution.py:194
  6.3 11.8 %collective-permute-start = (f32[4,4,48,256]{3,2,1,0:T(8,128)S(1)}, f32[4,4,48,256]{3,2,1,0:T(8,128)S(1)}, u32[]{:S(2)}, u32[]{:S(2)}) collective-permute-start(f32[4,4,48,256]{3,2,1,0:T(8,128)S(1)} %get-tuple-element.10), channel_id=1, source_target_pairs={{0,1},{1,0},{2,3},{3,2},{4,5},{5,4},{6,7},{7,6},{8,9},{9,8},{10,11... | collective-permute-start | bytes 2359304 | tf_op jit(solution)/shard_map/ppermute | solution.py:195
  8.8 9.5 %collective-permute-start.5 = (f32[4,48,256]{2,1,0:T(8,128)S(1)}, f32[4,48,256]{2,1,0:T(8,128)S(1)}, u32[]{:S(2)}, u32[]{:S(2)}) collective-permute-start(f32[4,48,256]{2,1,0:T(8,128)S(1)} %get-tuple-element.16), channel_id=1, source_target_pairs={{0,2},{1,5},{2,0},{3,7},{4,6},{5,1},{6,4},{7,3},{8,10},{9,13},{10,... | collective-permute-start | bytes 589832 | tf_op jit(solution)/shard_map/ppermute | solution.py:196
  12.3 12.0 %collective-permute-start.3 = (f32[2,4,48,256]{3,2,1,0:T(8,128)S(1)}, f32[2,4,48,256]{3,2,1,0:T(8,128)S(1)}, u32[]{:S(2)}, u32[]{:S(2)}) collective-permute-start(f32[2,4,48,256]{3,2,1,0:T(8,128)S(1)} %slice_add_fusion), channel_id=1, source_target_pairs={{0,2},{1,5},{2,0},{3,7},{4,6},{5,1},{6,4},{7,3},{8,10},{9,13},{10,... | collective-permute-start | bytes 1179656 | tf_op jit(solution)/shard_map/ppermute | solution.py:197
  14.7 16.1 %collective-permute-start.2 = (f32[4,48,256]{2,1,0:T(8,128)S(1)}, f32[4,48,256]{2,1,0:T(8,128)S(1)}, u32[]{:S(2)}, u32[]{:S(2)}) collective-permute-start(f32[4,48,256]{2,1,0:T(8,128)S(1)} %get-tuple-element.17), channel_id=1, source_target_pairs={{0,2},{1,5},{2,0},{3,7},{4,6},{5,1},{6,4},{7,3},{8,10},{9,13},{10,... | collective-permute-start | bytes 589832 | tf_op jit(solution)/shard_map/ppermute | solution.py:198
  18.1 43.4 %copy-start = (bf16[2,256,256]{2,1,0:T(8,128)(2,1)S(1)}, bf16[2,256,256]{2,1,0:T(8,128)(2,1)}, u32[]{:S(2)}) copy-start(bf16[2,256,256]{2,1,0:T(8,128)(2,1)} %constant.7.clone.table_ref) | copy-start | bytes 786436
  18.2 43.4 %copy-start.1 = (f32[1,48,256]{2,1,0:T(8,128)S(1)}, f32[1,48,256]{2,1,0:T(8,128)}, u32[]{:S(2)}) copy-start(f32[1,48,256]{2,1,0:T(8,128)} %param.7) | copy-start | bytes 147460
  18.3 10.6 %collective-permute-start.6 = (f32[4,48,256]{2,1,0:T(8,128)S(1)}, f32[4,48,256]{2,1,0:T(8,128)S(1)}, u32[]{:S(2)}, u32[]{:S(2)}) collective-permute-start(f32[4,48,256]{2,1,0:T(8,128)S(1)} %fusion.1), channel_id=1, source_target_pairs={{0,4},{1,61},{2,6},{3,63},{4,0},{5,9},{6,2},{7,11},{8,12},{9,5},{1... | collective-permute-start | bytes 589832 | tf_op jit(solution)/shard_map/ppermute | solution.py:199
  24.3 7.6 %collective-permute-start.4 = (f32[4,48,256]{2,1,0:T(8,128)S(1)}, f32[4,48,256]{2,1,0:T(8,128)S(1)}, u32[]{:S(2)}, u32[]{:S(2)}) collective-permute-start(f32[4,48,256]{2,1,0:T(8,128)S(1)} %get-tuple-element.19), channel_id=1, source_target_pairs={{0,4},{1,61},{2,6},{3,63},{4,0},{5,9},{6,2},{7,11},{8,12},{9,5},{1... | collective-permute-start | bytes 589832 | tf_op jit(solution)/shard_map/ppermute | solution.py:201
  28.9 7.6 %collective-permute-start.7 = (f32[4,48,256]{2,1,0:T(8,128)S(1)}, f32[4,48,256]{2,1,0:T(8,128)S(1)}, u32[]{:S(2)}, u32[]{:S(2)}) collective-permute-start(f32[4,48,256]{2,1,0:T(8,128)S(1)} %add.38), channel_id=1, source_target_pairs={{0,60},{1,3},{2,62},{3,1},{4,8},{5,7},{6,10},{7,5},{8,4},{9,11},{1... | collective-permute-start | bytes 589832 | tf_op jit(solution)/shard_map/ppermute | solution.py:202
